TPU v7x, 1024 devices: a whole 8x8x8 slice. The times are simulated.
1024 devices in a mesh: row: 256 (over y_lo, x, z, core), col: 4 (over y_hi).
Axes of the slice: x: 8, y: 8 (y_hi: 4, y_lo: 2; y = y_hi * 2 + y_lo), z: 8, core: 2. Of those that a mesh axis runs over, the one named last changes fastest.
Arguments:
- features: bfloat16 [262144, 512], P('row', 'col'), may hold values from -6 to 6
- tile_vals: bfloat16 [2048, 16, 128, 128], P('row'), may hold values from -0.4375 to 0.4375
- tile_cols: int32 [2048, 16], P('row'), may hold values from 0 to 2047, as said below
- tile_count: int32 [2048], P('row'), may hold values from 2 to 16
- weight: bfloat16 [512, 512], P('col'), may hold values from -0.25 to 0.25
- cotangent: bfloat16 [262144, 512], P('row'), may hold values from -6 to 6
Outputs:
- activated: bfloat16 [262144, 512], P('row', 'col')
- grad_weight: float32 [512, 512], P('col')
Inputs may be any that keep to these rules, and one draw needn't show every extreme that they name: Block tile_cols[b, t] is held by a device at most 4 indices away from the one holding row block b: tile_cols[b, t] // 8 - b // 8 lies in -4 to 4. Blocks may repeat within a row block; slots at or beyond tile_count[b] hold valid ids and carry no weight.
All inputs are finite; a program needn't handle non-finite values.
Results may differ from a plain program's by a relative error of at most 0.017.
Values may be sent and summed in bfloat16 or wider, within the bound.
No kernel may reach another device: no remote copies, remote signals or barrier semaphores. Data moves between devices by JAX's collectives and lax.ppermute only.
A program may use at most 32 MiB of HBM per device.

v0:
```python
import jax
import jax.numpy as jnp
from jax import lax
from jax.sharding import PartitionSpec as P

BAND = 4


def passed_along(x, axis, by):
    devices = lax.axis_size(axis)
    pairs = [(i, i + by) for i in range(devices) if 0 <= i + by < devices]
    return lax.ppermute(x, axis, pairs)


def shards(features, tile_vals, tile_cols, tile_count, weight, cotangent):
    rows_here = features.shape[0]
    feat_cols = features.shape[1]
    blocks_here = tile_vals.shape[0]
    slots = tile_vals.shape[1]
    tile = tile_vals.shape[2]
    device = lax.axis_index("row")
    pieces = []
    for offset in range(-BAND, BAND + 1):
        if offset == 0:
            pieces.append(features[None])
        else:
            pieces.append(passed_along(features[None], "row", -offset))
    window = jnp.concatenate(pieces, axis=0)
    window_blocks = window.reshape((2 * BAND + 1) * blocks_here, tile, feat_cols)
    local_ids = tile_cols - (device - BAND) * blocks_here
    picked = window_blocks[local_ids]
    keep = jnp.arange(slots, dtype=jnp.int32)[None, :] < tile_count[:, None]
    picked = jnp.where(keep[:, :, None, None], picked, jnp.zeros((), picked.dtype))
    summed = jnp.einsum("btij,btjf->bif", tile_vals, picked, preferred_element_type=jnp.float32)
    aggregated = summed.reshape(rows_here, feat_cols).astype(jnp.bfloat16)
    partial_value = jnp.dot(aggregated, weight, preferred_element_type=jnp.float32)
    out_cols = cotangent.shape[1] // lax.axis_size("col")
    start = lax.axis_index("col") * out_cols
    pre = lax.psum(partial_value.astype(jnp.bfloat16), "col").astype(jnp.float32)
    sigma = jax.nn.sigmoid(pre)
    activated = lax.dynamic_slice_in_dim(pre * sigma, start, out_cols, 1).astype(jnp.bfloat16)
    dpre = (cotangent.astype(jnp.float32) * sigma * (1.0 + pre * (1.0 - sigma))).astype(
        jnp.bfloat16
    )
    local_grad = lax.dot_general(
        aggregated, dpre, (((0,), (0,)), ((), ())), preferred_element_type=jnp.float32
    )
    grad_weight = lax.psum(local_grad, "row")
    return (activated, grad_weight)


def solution(mesh):
    return jax.shard_map(
        shards,
        mesh=mesh,
        in_specs=(
            P("row", "col"),
            P("row", None, None, None),
            P("row", None),
            P("row"),
            P("col", None),
            P("row", None),
        ),
        out_specs=(P("row", "col"), P("col", None)),
        check_vma=False,
    )
```

profile of v0, /device:TPU:1, one launch (start us, length us, event | category | flops | bytes accessed | tf_op | source)
XLA Modules:
  0.0 2039.9 jit_solution(9675782176525251531)
XLA Ops:
  7.2 8.5 collective-permute-start
  15.7 9.7 collective-permute-start.1
  25.4 4.0 collective-permute-start.2
  29.4 1.9 collective-permute-start.3
  31.3 2.4 collective-permute-start.4
  33.8 0.7 compare_select_fusion
  34.5 0.7 iota_compare_fusion
  35.3 0.7 copy-done.2
  36.0 1.3 collective-permute-start.5
  37.3 1.0 constant_dynamic-update-slice_fusion.8
  38.3 1.3 collective-permute-start.6
  39.6 1.3 collective-permute-start.7
  41.0 1.0 constant_dynamic-update-slice_fusion.4
  42.1 4.8 collective-permute-done.5
  46.9 9.6 collective-permute-done.6
  56.5 12.2 collective-permute-done.7
  68.8 3.0 gather_fusion
  71.8 4.8 fusion.7
  76.6 1.4 convolution_convert_fusion
  78.1 81.7 %all-reduce.3.cloned.1.call-done = bf16[1024,512]{1,0:T(8,128)(2,1)} async-done(((bf16[1024,512]{1,0:T(8,128)(2,1)}), bf16[1024,512]{1,0:T(8,128)(2,1)}) %all-reduce.3.cloned.1.call-update) | async-done | bytes 1048592 | tf_op jit(solution)/shard_map/psum | solution.py:39
  159.9 3.1 fusion.10
  163.8 0.8 fusion.11
  164.7 1866.7 %all-reduce.5.cloned.1.call-done = f32[128,512]{1,0:T(8,128)} async-done(((f32[128,512]{1,0:T(8,128)}), f32[128,512]{1,0:T(8,128)}) %all-reduce.5.cloned.1.call-update) | async-done | bytes 262160 | tf_op jit(solution)/shard_map/psum | solution.py:48
  2031.4 1.7 copy.19
  (27 shorter events, 1.3 us)
Async XLA Ops:
  7.2 69.4 %copy-start = (bf16[128,512]{1,0:T(8,128)(2,1)S(1)}, bf16[128,512]{1,0:T(8,128)(2,1)}, u32[]{:S(2)}) copy-start(bf16[128,512]{1,0:T(8,128)(2,1)} %param.10) | copy-start | bytes 393220
  7.2 152.7 %all-reduce.3.cloned.1.call-start = ((), (), s32[]{:S(2)}) async-start(), calls=%async_computation | async-start | bytes 2097152 | tf_op jit(solution)/shard_map/psum | solution.py:39
  7.2 28.1 %collective-permute-start = (bf16[1,1024,128]{2,1,0:T(8,128)(2,1)}, bf16[1,1024,128]{2,1,0:T(8,128)(2,1)S(1)}, u32[]{:S(2)}, u32[]{:S(2)}) collective-permute-start(bf16[1,1024,128]{2,1,0:T(8,128)(2,1)} %bitcast.18), channel_id=1, source_target_pairs={{0,16},{4,20},{8,24},{12,28},{16,32},{20,36},{24,40},{28,44},{32,4... | collective-permute-start | bytes 786440 | tf_op jit(solution)/shard_map/ppermute | solution.py:12
  15.7 22.6 %collective-permute-start.1 = (bf16[1,1024,128]{2,1,0:T(8,128)(2,1)}, bf16[1,1024,128]{2,1,0:T(8,128)(2,1)S(1)}, u32[]{:S(2)}, u32[]{:S(2)}) collective-permute-start(bf16[1,1024,128]{2,1,0:T(8,128)(2,1)} %bitcast.19), channel_id=1, source_target_pairs={{0,12},{4,16},{8,20},{12,24},{16,28},{20,32},{24,36},{28,40},{32,4... | collective-permute-start | bytes 786440 | tf_op jit(solution)/shard_map/ppermute | solution.py:12
  25.4 14.2 collective-permute-start.2
  29.4 11.6 collective-permute-start.3
  31.3 10.7 collective-permute-start.4
  35.3 0.7 copy-start.2
  36.0 10.8 collective-permute-start.5
  38.3 18.2 collective-permute-start.6
  39.6 29.1 %collective-permute-start.7 = (bf16[1,1024,128]{2,1,0:T(8,128)(2,1)}, bf16[1,1024,128]{2,1,0:T(8,128)(2,1)S(1)}, u32[]{:S(2)}, u32[]{:S(2)}) collective-permute-start(bf16[1,1024,128]{2,1,0:T(8,128)(2,1)} %bitcast.25), channel_id=1, source_target_pairs={{16,0},{20,4},{24,8},{28,12},{32,16},{36,20},{40,24},{44,28},{48,3... | collective-permute-start | bytes 786440 | tf_op jit(solution)/shard_map/ppermute | solution.py:12
  76.6 83.3 %copy-start.3 = (bf16[1024,512]{1,0:T(8,128)(2,1)S(1)}, bf16[1024,512]{1,0:T(8,128)(2,1)}, u32[]{:S(2)}) copy-start(bf16[1024,512]{1,0:T(8,128)(2,1)} %param.11) | copy-start | bytes 3145732
  78.1 1953.3 %all-reduce.5.cloned.1.call-start = ((), (), s32[]{:S(2)}) async-start(), calls=%async_computation.1 | async-start | bytes 524288 | tf_op jit(solution)/shard_map/psum | solution.py:48
  159.9 3.1 copy-start.1
Sparse Core Ops, SparseCore 0:
  78.2 81.6 all-reduce.2
  164.3 1867.0 all-reduce.4
where the time goes:
time: 2040 us
  waiting for transfers between devices  1980 us (97%)
  starting transfers between devices  30.5 us (1%)
    psum x1, waiting for transfers between devices, shards(): grad_weight = lax.psum(local_grad, 'row')  1870 us
    psum x1, waiting for transfers between devices, shards(): lax.psum(partial_value.astype(jnp.bfloat16), 'col').astype(jnp.float32)  81.7 us
  transfers between devices with their start and end apart: 10, of which 5 were waited for; matrix products, arithmetic and copies ran while one was open for 0% of the time, Pallas kernels for 0%

commit v1 on v0

v1 whole, which is shorter than its diff:
```python
import functools

import jax
import jax.numpy as jnp
from jax import lax
from jax.experimental import pallas as pl
from jax.experimental.pallas import tpu as pltpu
from jax.sharding import Mesh, PartitionSpec as P

ROW = ("y_lo", "x", "z", "core")
NEAR = ("z", "core")
FAR = ("y_lo", "x")
F32 = jnp.float32
BF16 = jnp.bfloat16


def shifted(x, by):
    n = lax.axis_size(ROW)
    return lax.ppermute(x, ROW, [(i + by, i) for i in range(n) if 0 <= i + by < n])


def swapped(x):
    return lax.ppermute(x, "core", [(0, 1), (1, 0)])


def halo(features):
    left2, right2 = shifted(features, -4), shifted(features, 4)
    left, right = shifted(features, -2), shifted(features, 2)
    others = swapped(jnp.stack([left, features, right]))
    core = lax.axis_index("core")
    edge = swapped(jnp.where(core == 0, right2, left2))
    return [(left2, 0), (left, 1), (features, 2), (right, 3), (right2, 4), (others, 5), (edge, 8)]


def slots_of(tile_cols, tile_count, blocks_here):
    device = lax.axis_index(ROW)
    source = tile_cols // blocks_here
    chip = source // 2 - device // 2
    same = source % 2 == device % 2
    other = jnp.where(jnp.abs(chip) == 2, 8, chip + 6)
    group = jnp.where(same, chip + 2, other)
    slot = group * blocks_here + tile_cols % blocks_here
    keep = jnp.arange(tile_cols.shape[1], dtype=jnp.int32)[None, :] < tile_count[:, None]
    return jnp.where(keep, slot, 9 * blocks_here)


def tiles_kernel(starts, slots, *refs):
    pieces = refs[: len(starts)]
    vals_hbm, out, window, vals, piece_sems, vals_sems = refs[len(starts) :]
    blocks, count, tile, cols = vals.shape[0], vals.shape[1], vals.shape[2], window.shape[2]
    copies = [
        pltpu.make_async_copy(piece, window.at[pl.ds(start, piece.shape[0])], piece_sems.at[i])
        for i, (piece, start) in enumerate(zip(pieces, starts))
    ]
    for copy in copies:
        copy.start()
    fetches = [
        pltpu.make_async_copy(vals_hbm.at[b], vals.at[b], vals_sems.at[b]) for b in range(blocks)
    ]
    for fetch in fetches:
        fetch.start()
    window[window.shape[0] - 1] = jnp.zeros((tile, cols), window.dtype)
    for copy in copies:
        copy.wait()
    for b in range(blocks):
        fetches[b].wait()
        total = jnp.zeros((tile, cols), F32)
        for t in range(0, count, 2):
            pair = jnp.concatenate([vals[b, t], vals[b, t + 1]], axis=1)
            rows = jnp.concatenate([window[slots[b, t]], window[slots[b, t + 1]]], axis=0)
            total += jnp.dot(pair, rows, preferred_element_type=F32)
        out[pl.ds(b * tile, tile), :] = total.astype(out.dtype)


def tiles(pieces, slots, tile_vals):
    blocks, count, tile, _ = tile_vals.shape
    cols = pieces[0][0].shape[-1]
    arrays = [x.reshape(-1, tile, cols) for x, _ in pieces]
    starts = [group * blocks for _, group in pieces]
    hbm = pl.BlockSpec(memory_space=pl.ANY)
    return pl.pallas_call(
        functools.partial(tiles_kernel, starts),
        out_shape=jax.ShapeDtypeStruct((blocks * tile, cols), BF16),
        in_specs=[pl.BlockSpec(memory_space=pltpu.SMEM)] + [hbm] * (len(arrays) + 1),
        out_specs=pl.BlockSpec(memory_space=pltpu.VMEM),
        scratch_shapes=[
            pltpu.VMEM((9 * blocks + 1, tile, cols), BF16),
            pltpu.VMEM(tile_vals.shape, BF16),
            pltpu.SemaphoreType.DMA((len(arrays),)),
            pltpu.SemaphoreType.DMA((blocks,)),
        ],
        compiler_params=pltpu.CompilerParams(vmem_limit_bytes=16 << 20),
        cost_estimate=pl.CostEstimate(
            flops=2 * blocks * count * tile * tile * cols, bytes_accessed=7 << 20, transcendentals=0
        ),
    )(slots, *arrays, tile_vals)


def dense_kernel(me, agg, weight, cotangent, activated, grad, act, total):
    step = pl.program_id(0)
    mine = me[0]
    width = activated.shape[1]
    joined = jnp.concatenate([agg[k] for k in range(agg.shape[0])], axis=1)
    pre = jnp.dot(joined, weight[...], preferred_element_type=F32)
    sigma = 0.5 * jnp.tanh(0.5 * pre) + 0.5
    act[...] = pre * sigma
    activated[...] = act[:, pl.ds(pl.multiple_of(mine * width, width), width)].astype(BF16)
    dpre = (cotangent[...].astype(F32) * sigma * (1.0 + pre * (1.0 - sigma))).astype(BF16)
    part = lax.dot_general(agg[mine], dpre, (((0,), (0,)), ((), ())), preferred_element_type=F32)

    @pl.when(step == 0)
    def _():
        total[...] = part

    @pl.when(step > 0)
    def _():
        total[...] += part

    @pl.when(step == pl.num_programs(0) - 1)
    def _():
        grad[...] = total[...].astype(BF16)


def dense(agg, weight, cotangent):
    groups, rows, width = agg.shape
    f_out = weight.shape[1]
    block = 256
    me = lax.axis_index("col").astype(jnp.int32)[None]
    return pl.pallas_call(
        dense_kernel,
        out_shape=(
            jax.ShapeDtypeStruct((rows, f_out // groups), BF16),
            jax.ShapeDtypeStruct((width, f_out), BF16),
        ),
        grid=(rows // block,),
        in_specs=[
            pl.BlockSpec(memory_space=pltpu.SMEM),
            pl.BlockSpec((groups, block, width), lambda i: (0, i, 0)),
            pl.BlockSpec((groups * width, f_out), lambda i: (0, 0)),
            pl.BlockSpec((block, f_out), lambda i: (i, 0)),
        ],
        out_specs=(
            pl.BlockSpec((block, f_out // groups), lambda i: (i, 0)),
            pl.BlockSpec((width, f_out), lambda i: (0, 0)),
        ),
        scratch_shapes=[pltpu.VMEM((block, f_out), F32), pltpu.VMEM((width, f_out), F32)],
        compiler_params=pltpu.CompilerParams(vmem_limit_bytes=16 << 20),
    )(me, agg, weight, cotangent)


def spread(x, axes):
    n = lax.axis_size(axes)
    return lax.all_to_all(jnp.broadcast_to(x[None], (n,) + x.shape), axes, 0, 0, tiled=True)


def summed_over_row(part):
    near = lax.axis_size(NEAR)
    rows, cols = part.shape
    pieces = lax.all_to_all(part.reshape(near, rows // near, cols), NEAR, 0, 0, tiled=True)
    piece = jnp.sum(pieces.astype(F32), 0).astype(BF16)
    whole = jnp.sum(spread(piece, FAR).astype(F32), 0).astype(BF16)
    return spread(whole, NEAR).reshape(rows, cols).astype(F32)


def shards(features, tile_vals, tile_cols, tile_count, weight, cotangent):
    whole_weight = lax.all_gather(weight, "col", axis=0, tiled=True)
    slots = slots_of(tile_cols, tile_count, tile_vals.shape[0])
    aggregated = tiles(halo(features), slots, tile_vals)
    activated, part = dense(spread(aggregated, "col"), whole_weight, cotangent)
    return activated, summed_over_row(part)


def solution(mesh):
    split = Mesh(mesh.devices.reshape(2, 8, 8, 2, 4), ROW + ("col",))
    return jax.shard_map(
        shards,
        mesh=split,
        in_specs=(
            P(ROW, "col"),
            P(ROW, None, None, None),
            P(ROW, None),
            P(ROW),
            P("col", None),
            P(ROW, None),
        ),
        out_specs=(P(ROW, "col"), P("col", None)),
        check_vma=False,
    )
```

time: 2040 us -> 155 us (0.08)
  waiting for transfers between devices: 1980 us -> 23.5 us
  blocking collectives: 0 us -> 82.7 us
    psum x2 -> x0, waiting for transfers between devices: 1950 us -> none  [the longest x1 1870 us: shards(): grad_weight = lax.psum(local_grad, 'row')]
    all_to_all x0 -> x3, blocking collectives: none -> 46.3 us  [the longest x2 26.5 us: spread(): lax.all_to_all(jnp.broadcast_to(x[None], (n,) + x.shape), axes, 0, 0, til...]
    all_gather x0 -> x1, blocking collectives: none -> 36.4 us  [shards(): whole_weight = lax.all_gather(weight, 'col', axis=0, tiled=True)]
  transfers between devices with their start and end apart: 10 -> 7, of which waited for: 5 -> 5; matrix products, arithmetic and copies ran while one was open for 0% -> 1% of each run, Pallas kernels for 0% -> 0%
where the time goes in v1:
time: 155 us; the launch traced here: 154 us
  blocking collectives  82.7 us (53%)
  starting transfers between devices  33.5 us (22%)
  waiting for transfers between devices  23.5 us (15%)
  Pallas kernels  6.8 us (4%)
  local copies, waits for them, and re-layouts  4.27 us (3%)
  other arithmetic  2.61 us (2%)
    all_gather x1, blocking collectives, shards(): whole_weight = lax.all_gather(weight, 'col', axis=0, tiled=True)  36.4 us
    all_to_all x2, blocking collectives, spread(): lax.all_to_all(jnp.broadcast_to(x[None], (n,) + x.shape), axes, 0, 0, til...  26.5 us
    ppermute x4, waiting for transfers between devices, shifted(): lax.ppermute(x, ROW, [(i + by, i) for i in range(n) if 0 <= i + by < n])  23.1 us
    all_to_all x1, blocking collectives, summed_over_row(): lax.all_to_all(part.reshape(near, rows // near, cols), NEAR, 0, 0, tiled=...  19.8 us
    ppermute x2, starting transfers between devices, swapped(): return lax.ppermute(x, 'core', [(0, 1), (1, 0)])  14.9 us
    ppermute x4, starting transfers between devices, shifted(): lax.ppermute(x, ROW, [(i + by, i) for i in range(n) if 0 <= i + by < n])  11.4 us
    all_to_all x1, starting transfers between devices, spread(): lax.all_to_all(jnp.broadcast_to(x[None], (n,) + x.shape), axes, 0, 0, til...  7.27 us
    pallas_call x1, Pallas kernels, tiles(): pl.pallas_call(functools.partial(tiles_kernel, starts), out_shape=jax.Sha...  3.55 us
  transfers between devices with their start and end apart: 7, of which 5 were waited for; matrix products, arithmetic and copies ran while one was open for 1% of the time, Pallas kernels for 0%

profile of v1, /device:TPU:1, one launch (start us, length us, event | category | flops | bytes accessed | tf_op | source)
XLA Modules:
  0.0 154.1 jit_solution(3969500006854252811)
XLA Ops:
  0.6 5.8 %collective-permute-start.1 = (bf16[1024,128]{1,0:T(8,128)(2,1)}, bf16[1024,128]{1,0:T(8,128)(2,1)S(1)}, u32[]{:S(2)}, u32[]{:S(2)}) collective-permute-start(bf16[1024,128]{1,0:T(8,128)(2,1)} %param.6), channel_id=1, source_target_pairs={{0,8},{4,12},{8,16},{12,20},{16,24},{20,28},{24,32},{28,36},{32,40... | collective-permute-start | bytes 786440 | tf_op jit(solution)/shard_map/ppermute | solution.py:19
  6.4 1.3 collective-permute-start.2
  7.7 2.3 %collective-permute-done.1 = bf16[1024,128]{1,0:T(8,128)(2,1)S(1)} collective-permute-done((bf16[1024,128]{1,0:T(8,128)(2,1)}, bf16[1024,128]{1,0:T(8,128)(2,1)S(1)}, u32[]{:S(2)}, u32[]{:S(2)}) %collective-permute-start.1) | collective-permute-done | bytes 262176 | tf_op jit(solution)/shard_map/ppermute | solution.py:19
  10.0 5.3 %collective-permute-done.2 = bf16[1024,128]{1,0:T(8,128)(2,1)S(1)} collective-permute-done((bf16[1024,128]{1,0:T(8,128)(2,1)}, bf16[1024,128]{1,0:T(8,128)(2,1)S(1)}, u32[]{:S(2)}, u32[]{:S(2)}) %collective-permute-start.2) | collective-permute-done | bytes 262176 | tf_op jit(solution)/shard_map/ppermute | solution.py:19
  15.3 1.0 pad_maximum_fusion
  16.3 11.2 %collective-permute-start.4 = (bf16[3,1024,128]{2,1,0:T(8,128)(2,1)S(1)}, bf16[3,1024,128]{2,1,0:T(8,128)(2,1)S(1)}, u32[]{:S(2)}, u32[]{:S(2)}) collective-permute-start(bf16[3,1024,128]{2,1,0:T(8,128)(2,1)S(1)} %pad_maximum_fusion), channel_id=1, source_target_pairs={{0,4},{4,0},{1,5},{5,1},{2,6},{6,2},{3,7},{7,3},{8,12},{12,8},{9,1... | collective-permute-start | bytes 2359304 | tf_op jit(solution)/shard_map/ppermute | solution.py:23
  27.5 3.0 %collective-permute-start = (bf16[1024,128]{1,0:T(8,128)(2,1)}, bf16[1024,128]{1,0:T(8,128)(2,1)S(1)}, u32[]{:S(2)}, u32[]{:S(2)}) collective-permute-start(bf16[1024,128]{1,0:T(8,128)(2,1)} %param.6), channel_id=1, source_target_pairs={{0,16},{4,20},{8,24},{12,28},{16,32},{20,36},{24,40},{28,44},{32,4... | collective-permute-start | bytes 786440 | tf_op jit(solution)/shard_map/ppermute | solution.py:19
  30.6 1.3 collective-permute-start.3
  31.9 4.7 %collective-permute-done = bf16[1024,128]{1,0:T(8,128)(2,1)S(1)} collective-permute-done((bf16[1024,128]{1,0:T(8,128)(2,1)}, bf16[1024,128]{1,0:T(8,128)(2,1)S(1)}, u32[]{:S(2)}, u32[]{:S(2)}) %collective-permute-start) | collective-permute-done | bytes 262176 | tf_op jit(solution)/shard_map/ppermute | solution.py:19
  36.6 10.8 %collective-permute-done.3 = bf16[1024,128]{1,0:T(8,128)(2,1)S(1)} collective-permute-done((bf16[1024,128]{1,0:T(8,128)(2,1)}, bf16[1024,128]{1,0:T(8,128)(2,1)S(1)}, u32[]{:S(2)}, u32[]{:S(2)}) %collective-permute-start.3) | collective-permute-done | bytes 262176 | tf_op jit(solution)/shard_map/ppermute | solution.py:19
  47.4 3.7 %collective-permute-start.5 = (bf16[1024,128]{1,0:T(8,128)(2,1)S(1)}, bf16[1024,128]{1,0:T(8,128)(2,1)S(1)}, u32[]{:S(2)}, u32[]{:S(2)}) collective-permute-start(bf16[1024,128]{1,0:T(8,128)(2,1)S(1)} %broadcast_select_fusion), channel_id=1, source_target_pairs={{0,4},{4,0},{1,5},{5,1},{2,6},{6,2},{3,7},{7,3},{8,12},{12,8},{9,1... | collective-permute-start | bytes 786440 | tf_op jit(solution)/shard_map/ppermute | solution.py:23
  51.1 0.8 fusion.3.slots
  51.9 0.3 collective-permute-done.5
  52.3 2.2 %copy-done = bf16[8,16,128,128]{3,2,1,0:T(8,128)(2,1)S(1)} copy-done((bf16[8,16,128,128]{3,2,1,0:T(8,128)(2,1)S(1)}, bf16[8,16,128,128]{3,2,1,0:T(8,128)(2,1)}, u32[]{:S(2)}) %copy-start) | copy-done | bytes 4194328
  54.5 0.9 copy-done.2
  55.4 3.5 %shard_map.77 = bf16[1024,128]{1,0:T(8,128)(2,1)S(1)} custom-call(s32[8,16]{1,0:T(8,128)S(1)} %fusion.3.slots, bf16[8,128,128]{2,1,0:T(8,128)(2,1)S(1)} %bitcast.21, bf16[8,128,128]{2,1,0:T(8,128)(2,1)S(1)} %bitcast.18, bf16[8,128,128]{2,1,0:T(8,128)(2,1)S(1)} %bitcast.16, bf16[8,128,128]{2,1,0:T(8,128)(2,1)S(1)} %bitcast.20, ...), custom_call_target="tpu_custom_call" | custom-call | flops 536870912 | bytes 7340032 | tf_op jit(solution)/shard_map/pallas_call | solution.py:81
  59.0 1.1 broadcast_in_dim.16
  60.1 7.3 %all-to-all-start = ((bf16[4,1024,128]{2,1,0:T(8,128)(2,1)}), bf16[4,1024,128]{2,1,0:T(8,128)(2,1)S(1)}, u32[]{:S(2)}, u32[]{:S(2)}) async-start(bf16[4,1024,128]{2,1,0:T(8,128)(2,1)} %broadcast_in_dim.16), calls=%async_computation | async-start | bytes 2097152 | tf_op jit(solution)/shard_map/all_to_all | solution.py:153
  67.3 36.4 %all_gather.3.weight = bf16[512,512]{1,0:T(8,128)(2,1)S(1)} all-gather(bf16[128,512]{1,0:T(8,128)(2,1)S(1)} %copy-done.3), channel_id=1, replica_groups=mesh['y_lo'=2,'x'=8,'z'=8,'core'=2,'col'=4] {'col'}, dimensions={0}, use_global_device_ids=true | all-gather | bytes 655360 | tf_op jit(solution)/shard_map/all_gather | solution.py:166
  103.7 3.2 %shard_map.78 = (bf16[1024,128]{1,0:T(8,128)(2,1)}, bf16[128,512]{1,0:T(8,128)(2,1)S(1)}) custom-call(s32[1]{0:T(128)} %bitcast.me, bf16[4,1024,128]{2,1,0:T(8,128)(2,1)S(1)} %all-to-all-done.agg, bf16[512,512]{1,0:T(8,128)(2,1)S(1)} %all_gather.3.weight, bf16[1024,512]{1,0:T(8,128)(2,1)S(1)} %copy-done.1), custom_call_target="tpu_custom_call" | custom-call | tf_op jit(solution)/shard_map/pallas_call | solution.py:129
  107.0 19.8 %all_to_all.20 = bf16[16,8,512]{2,1,0:T(8,128)(2,1)S(1)} all-to-all(bf16[16,8,512]{2,1,0:T(8,128)(2,1)S(1)} %bitcast.25), channel_id=1, replica_groups=mesh['y_lo'=2,'x'=8,'z'=8,'core'=2,'col'=4] {'z','core'}, dimensions={0} | all-to-all | bytes 262144 | tf_op jit(solution)/shard_map/all_to_all | solution.py:159
  126.8 13.4 %all_to_all.21 = bf16[16,8,512]{2,1,0:T(8,128)(2,1)S(1)} all-to-all(bf16[16,8,512]{2,1,0:T(8,128)(2,1)S(1)} %broadcast_in_dim.17), channel_id=1, replica_groups=mesh['y_lo'=2,'x'=8,'z'=8,'core'=2,'col'=4] {'y_lo','x'}, dimensions={0} | all-to-all | bytes 262144 | tf_op jit(solution)/shard_map/all_to_all | solution.py:153
  140.3 13.1 %all_to_all.22 = bf16[16,8,512]{2,1,0:T(8,128)(2,1)S(1)} all-to-all(bf16[16,8,512]{2,1,0:T(8,128)(2,1)S(1)} %broadcast_in_dim.18), channel_id=1, replica_groups=mesh['y_lo'=2,'x'=8,'z'=8,'core'=2,'col'=4] {'z','core'}, dimensions={0} | all-to-all | bytes 262144 | tf_op jit(solution)/shard_map/all_to_all | solution.py:153
  153.4 0.7 bitcast_convert_fusion
  (13 shorter events, 0.1 us)
Async XLA Ops:
  0.6 9.4 %collective-permute-start.1 = (bf16[1024,128]{1,0:T(8,128)(2,1)}, bf16[1024,128]{1,0:T(8,128)(2,1)S(1)}, u32[]{:S(2)}, u32[]{:S(2)}) collective-permute-start(bf16[1024,128]{1,0:T(8,128)(2,1)} %param.6), channel_id=1, source_target_pairs={{0,8},{4,12},{8,16},{12,20},{16,24},{20,28},{24,32},{28,36},{32,40... | collective-permute-start | bytes 786440 | tf_op jit(solution)/shard_map/ppermute | solution.py:19
  6.4 8.9 %collective-permute-start.2 = (bf16[1024,128]{1,0:T(8,128)(2,1)}, bf16[1024,128]{1,0:T(8,128)(2,1)S(1)}, u32[]{:S(2)}, u32[]{:S(2)}) collective-permute-start(bf16[1024,128]{1,0:T(8,128)(2,1)} %param.6), channel_id=1, source_target_pairs={{8,0},{12,4},{16,8},{20,12},{24,16},{28,20},{32,24},{36,28},{40,32... | collective-permute-start | bytes 786440 | tf_op jit(solution)/shard_map/ppermute | solution.py:19
  16.3 36.0 %collective-permute-start.4 = (bf16[3,1024,128]{2,1,0:T(8,128)(2,1)S(1)}, bf16[3,1024,128]{2,1,0:T(8,128)(2,1)S(1)}, u32[]{:S(2)}, u32[]{:S(2)}) collective-permute-start(bf16[3,1024,128]{2,1,0:T(8,128)(2,1)S(1)} %pad_maximum_fusion), channel_id=1, source_target_pairs={{0,4},{4,0},{1,5},{5,1},{2,6},{6,2},{3,7},{7,3},{8,12},{12,8},{9,1... | collective-permute-start | bytes 2359304 | tf_op jit(solution)/shard_map/ppermute | solution.py:23
  27.5 9.1 %collective-permute-start = (bf16[1024,128]{1,0:T(8,128)(2,1)}, bf16[1024,128]{1,0:T(8,128)(2,1)S(1)}, u32[]{:S(2)}, u32[]{:S(2)}) collective-permute-start(bf16[1024,128]{1,0:T(8,128)(2,1)} %param.6), channel_id=1, source_target_pairs={{0,16},{4,20},{8,24},{12,28},{16,32},{20,36},{24,40},{28,44},{32,4... | collective-permute-start | bytes 786440 | tf_op jit(solution)/shard_map/ppermute | solution.py:19
  30.6 16.8 %collective-permute-start.3 = (bf16[1024,128]{1,0:T(8,128)(2,1)}, bf16[1024,128]{1,0:T(8,128)(2,1)S(1)}, u32[]{:S(2)}, u32[]{:S(2)}) collective-permute-start(bf16[1024,128]{1,0:T(8,128)(2,1)} %param.6), channel_id=1, source_target_pairs={{16,0},{20,4},{24,8},{28,12},{32,16},{36,20},{40,24},{44,28},{48,3... | collective-permute-start | bytes 786440 | tf_op jit(solution)/shard_map/ppermute | solution.py:19
  47.4 4.8 %collective-permute-start.5 = (bf16[1024,128]{1,0:T(8,128)(2,1)S(1)}, bf16[1024,128]{1,0:T(8,128)(2,1)S(1)}, u32[]{:S(2)}, u32[]{:S(2)}) collective-permute-start(bf16[1024,128]{1,0:T(8,128)(2,1)S(1)} %broadcast_select_fusion), channel_id=1, source_target_pairs={{0,4},{4,0},{1,5},{5,1},{2,6},{6,2},{3,7},{7,3},{8,12},{12,8},{9,1... | collective-permute-start | bytes 786440 | tf_op jit(solution)/shard_map/ppermute | solution.py:23
  52.3 2.2 %copy-start = (bf16[8,16,128,128]{3,2,1,0:T(8,128)(2,1)S(1)}, bf16[8,16,128,128]{3,2,1,0:T(8,128)(2,1)}, u32[]{:S(2)}) copy-start(bf16[8,16,128,128]{3,2,1,0:T(8,128)(2,1)} %refs_7_.1) | copy-start | bytes 12582916
  54.5 0.9 copy-start.2
  55.4 11.9 %copy-start.3 = (bf16[128,512]{1,0:T(8,128)(2,1)S(1)}, bf16[128,512]{1,0:T(8,128)(2,1)}, u32[]{:S(2)}) copy-start(bf16[128,512]{1,0:T(8,128)(2,1)} %param.10) | copy-start | bytes 393220
  55.4 48.3 %copy-start.1 = (bf16[1024,512]{1,0:T(8,128)(2,1)S(1)}, bf16[1024,512]{1,0:T(8,128)(2,1)}, u32[]{:S(2)}) copy-start(bf16[1024,512]{1,0:T(8,128)(2,1)} %cotangent.1) | copy-start | bytes 3145732
  60.1 43.6 %all-to-all-start = ((bf16[4,1024,128]{2,1,0:T(8,128)(2,1)}), bf16[4,1024,128]{2,1,0:T(8,128)(2,1)S(1)}, u32[]{:S(2)}, u32[]{:S(2)}) async-start(bf16[4,1024,128]{2,1,0:T(8,128)(2,1)} %broadcast_in_dim.16), calls=%async_computation | async-start | bytes 2097152 | tf_op jit(solution)/shard_map/all_to_all | solution.py:153

commit v2 on v1

--- a/solution.py
+++ b/solution.py
@@ -23,13 +23,16 @@
     return lax.ppermute(x, "core", [(0, 1), (1, 0)])
 
 
-def halo(features):
+def halo(features, weight):
+    whole_weight = spread(weight, "col")
     left2, right2 = shifted(features, -4), shifted(features, 4)
     left, right = shifted(features, -2), shifted(features, 2)
-    others = swapped(jnp.stack([left, features, right]))
     core = lax.axis_index("core")
-    edge = swapped(jnp.where(core == 0, right2, left2))
-    return [(left2, 0), (left, 1), (features, 2), (right, 3), (right2, 4), (others, 5), (edge, 8)]
+    edge = jnp.where(core == 0, right2, left2)
+    zero = whole_weight[0, 0, 0] * 0
+    others = swapped(jnp.stack([left, features, right, edge]) + zero)
+    pieces = [(left2, 0), (left, 1), (features, 2), (right, 3), (right2, 4), (others, 5)]
+    return pieces, whole_weight.reshape(-1, weight.shape[1])
 
 
 def slots_of(tile_cols, tile_count, blocks_here):
@@ -69,19 +72,23 @@
             pair = jnp.concatenate([vals[b, t], vals[b, t + 1]], axis=1)
             rows = jnp.concatenate([window[slots[b, t]], window[slots[b, t + 1]]], axis=0)
             total += jnp.dot(pair, rows, preferred_element_type=F32)
-        out[pl.ds(b * tile, tile), :] = total.astype(out.dtype)
-
-
-def tiles(pieces, slots, tile_vals):
+        done = total.astype(out.dtype)
+        for k in range(out.shape[0]):
+            out[k, pl.ds(b * tile, tile), :] = done
+
+
+def tiles(pieces, slots, tile_vals, times):
     blocks, count, tile, _ = tile_vals.shape
     cols = pieces[0][0].shape[-1]
     arrays = [x.reshape(-1, tile, cols) for x, _ in pieces]
+    arrays[2] = pltpu.with_memory_space_constraint(arrays[2], pltpu.HBM)
     starts = [group * blocks for _, group in pieces]
-    hbm = pl.BlockSpec(memory_space=pl.ANY)
+    anywhere = pl.BlockSpec(memory_space=pl.ANY)
+    hbm = pl.BlockSpec(memory_space=pltpu.HBM)
     return pl.pallas_call(
         functools.partial(tiles_kernel, starts),
-        out_shape=jax.ShapeDtypeStruct((blocks * tile, cols), BF16),
-        in_specs=[pl.BlockSpec(memory_space=pltpu.SMEM)] + [hbm] * (len(arrays) + 1),
+        out_shape=jax.ShapeDtypeStruct((times, blocks * tile, cols), BF16),
+        in_specs=[pl.BlockSpec(memory_space=pltpu.SMEM)] + [anywhere] * len(arrays) + [hbm],
         out_specs=pl.BlockSpec(memory_space=pltpu.VMEM),
         scratch_shapes=[
             pltpu.VMEM((9 * blocks + 1, tile, cols), BF16),
@@ -93,7 +100,7 @@
         cost_estimate=pl.CostEstimate(
             flops=2 * blocks * count * tile * tile * cols, bytes_accessed=7 << 20, transcendentals=0
         ),
-    )(slots, *arrays, tile_vals)
+    )(slots, *arrays, pltpu.with_memory_space_constraint(tile_vals, pltpu.HBM))
 
 
 def dense_kernel(me, agg, weight, cotangent, activated, grad, act, total):
@@ -150,23 +157,28 @@
 
 def spread(x, axes):
     n = lax.axis_size(axes)
-    return lax.all_to_all(jnp.broadcast_to(x[None], (n,) + x.shape), axes, 0, 0, tiled=True)
+    return exchanged(jnp.broadcast_to(x[None], (n,) + x.shape), axes)
+
+
+def exchanged(x, axes):
+    return lax.all_to_all(x, axes, 0, 0, tiled=True)
 
 
 def summed_over_row(part):
     near = lax.axis_size(NEAR)
     rows, cols = part.shape
-    pieces = lax.all_to_all(part.reshape(near, rows // near, cols), NEAR, 0, 0, tiled=True)
+    pieces = exchanged(part.reshape(near, rows // near, cols), NEAR)
     piece = jnp.sum(pieces.astype(F32), 0).astype(BF16)
     whole = jnp.sum(spread(piece, FAR).astype(F32), 0).astype(BF16)
     return spread(whole, NEAR).reshape(rows, cols).astype(F32)
 
 
 def shards(features, tile_vals, tile_cols, tile_count, weight, cotangent):
-    whole_weight = lax.all_gather(weight, "col", axis=0, tiled=True)
+    groups = lax.axis_size("col")
     slots = slots_of(tile_cols, tile_count, tile_vals.shape[0])
-    aggregated = tiles(halo(features), slots, tile_vals)
-    activated, part = dense(spread(aggregated, "col"), whole_weight, cotangent)
+    pieces, whole_weight = halo(features, weight)
+    aggregated = tiles(pieces, slots, tile_vals, groups)
+    activated, part = dense(exchanged(aggregated, "col"), whole_weight, cotangent)
     return activated, summed_over_row(part)
 
 

time: 155 us -> 142 us (0.916)
  blocking collectives: 82.7 us -> 57 us
  waiting for transfers between devices: 23.5 us -> 31 us
  starting transfers between devices: 33.5 us -> 37.4 us
  Pallas kernels: 6.8 us -> 8.49 us
    all_gather x1 -> x0, blocking collectives: 36.4 us -> none  [shards(): whole_weight = lax.all_gather(weight, 'col', axis=0, tiled=True)]
    all_to_all x1 -> x2, waiting for transfers between devices: 0.01 us -> 19.2 us  [exchanged(): return lax.all_to_all(x, axes, 0, 0, tiled=True)]
    ppermute x4, waiting for transfers between devices: 23.1 us -> 9.47 us  [shifted(): lax.ppermute(x, ROW, [(i + by, i) for i in range(n) if 0 <= i + by < n])]
    all_to_all x3, blocking collectives: 46.3 us -> 57 us  [exchanged(): return lax.all_to_all(x, axes, 0, 0, tiled=True)]
    ppermute x2 -> x1, starting transfers between devices: 14.9 us -> 6.96 us  [swapped(): return lax.ppermute(x, 'core', [(0, 1), (1, 0)])]
    all_to_all x1 -> x2, starting transfers between devices: 7.27 us -> 14.7 us  [exchanged(): return lax.all_to_all(x, axes, 0, 0, tiled=True)]
    ppermute x4, starting transfers between devices: 11.4 us -> 15.8 us  [shifted(): lax.ppermute(x, ROW, [(i + by, i) for i in range(n) if 0 <= i + by < n])]
    unnamed x8 -> x10, local copies, waits for them, and re-layouts: 3.15 us -> 0.97 us
  transfers between devices with their start and end apart: 7 -> 7, of which waited for: 5 -> 3; matrix products, arithmetic and copies ran while one was open for 1% -> 0% of each run, Pallas kernels for 0% -> 0%
where the time goes in v2:
time: 142 us
  blocking collectives  57 us (40%)
  starting transfers between devices  37.4 us (26%)
  waiting for transfers between devices  31 us (22%)
  Pallas kernels  8.49 us (6%)
  local copies, waits for them, and re-layouts  3.29 us (2%)
  other arithmetic  2.93 us (2%)
  between operations  1.47 us (1%)
    all_to_all x3, blocking collectives, exchanged(): return lax.all_to_all(x, axes, 0, 0, tiled=True)  57 us
    all_to_all x2, waiting for transfers between devices, exchanged(): return lax.all_to_all(x, axes, 0, 0, tiled=True)  19.2 us
    ppermute x4, starting transfers between devices, shifted(): lax.ppermute(x, ROW, [(i + by, i) for i in range(n) if 0 <= i + by < n])  15.8 us
    all_to_all x2, starting transfers between devices, exchanged(): return lax.all_to_all(x, axes, 0, 0, tiled=True)  14.7 us
    ppermute x4, waiting for transfers between devices, shifted(): lax.ppermute(x, ROW, [(i + by, i) for i in range(n) if 0 <= i + by < n])  9.47 us
    ppermute x1, starting transfers between devices, swapped(): return lax.ppermute(x, 'core', [(0, 1), (1, 0)])  6.96 us
    pallas_call x1, Pallas kernels, tiles(): pl.pallas_call(functools.partial(tiles_kernel, starts), out_shape=jax.Sha...  5.25 us
    pallas_call x1, Pallas kernels, dense(): pl.pallas_call(dense_kernel, out_shape=(jax.ShapeDtypeStruct((rows, f_out...  3.24 us
  transfers between devices with their start and end apart: 7, of which 3 were waited for; matrix products, arithmetic and copies ran while one was open for 0% of the time, Pallas kernels for 0%

profile of v2, /device:TPU:1, one launch (start us, length us, event | category | flops | bytes accessed | tf_op | source)
XLA Modules:
  0.0 141.6 jit_solution(1804692455816332230)
XLA Ops:
  0.7 1.8 %broadcast_in_dim.16 = bf16[4,128,512]{2,1,0:T(8,128)(2,1)} broadcast(bf16[128,512]{1,0:T(8,128)(2,1)} %param.10), dimensions={1,2} | broadcast | bytes 655360 | tf_op jit(solution)/shard_map/broadcast_in_dim | solution.py:160
  2.4 8.1 %all-to-all-start = ((bf16[4,128,512]{2,1,0:T(8,128)(2,1)}), bf16[4,128,512]{2,1,0:T(8,128)(2,1)S(1)}, u32[]{:S(2)}, u32[]{:S(2)}) async-start(bf16[4,128,512]{2,1,0:T(8,128)(2,1)} %broadcast_in_dim.16), calls=%async_computation | async-start | bytes 1048576 | tf_op jit(solution)/shard_map/all_to_all | solution.py:164
  10.5 7.6 %collective-permute-start = (bf16[1024,128]{1,0:T(8,128)(2,1)}, bf16[1024,128]{1,0:T(8,128)(2,1)S(1)}, u32[]{:S(2)}, u32[]{:S(2)}) collective-permute-start(bf16[1024,128]{1,0:T(8,128)(2,1)} %param.6), channel_id=1, source_target_pairs={{0,16},{4,20},{8,24},{12,28},{16,32},{20,36},{24,40},{28,44},{32,4... | collective-permute-start | bytes 786440 | tf_op jit(solution)/shard_map/ppermute | solution.py:19
  18.1 1.3 collective-permute-start.3
  19.4 1.3 collective-permute-start.2
  20.7 5.6 %collective-permute-start.1 = (bf16[1024,128]{1,0:T(8,128)(2,1)}, bf16[1024,128]{1,0:T(8,128)(2,1)S(1)}, u32[]{:S(2)}, u32[]{:S(2)}) collective-permute-start(bf16[1024,128]{1,0:T(8,128)(2,1)} %param.6), channel_id=1, source_target_pairs={{0,8},{4,12},{8,16},{12,20},{16,24},{20,28},{24,32},{28,36},{32,40... | collective-permute-start | bytes 786440 | tf_op jit(solution)/shard_map/ppermute | solution.py:19
  26.3 0.0 collective-permute-done
  26.3 9.5 %collective-permute-done.3 = bf16[1024,128]{1,0:T(8,128)(2,1)S(1)} collective-permute-done((bf16[1024,128]{1,0:T(8,128)(2,1)}, bf16[1024,128]{1,0:T(8,128)(2,1)S(1)}, u32[]{:S(2)}, u32[]{:S(2)}) %collective-permute-start.3) | collective-permute-done | bytes 262176 | tf_op jit(solution)/shard_map/ppermute | solution.py:19
  35.8 0.0 all-to-all-done
  35.8 0.6 slice.4
  37.0 0.0 collective-permute-done.2
  37.1 2.1 %maximum_add_fusion = bf16[4,1024,128]{2,1,0:T(8,128)(2,1)} fusion(bf16[1,1024,128]{2,1,0:T(8,128)(2,1)S(1)} %select_bitcast_fusion, bf16[1,1024,128]{2,1,0:T(8,128)(2,1)S(1)} %bitcast.20, bf16[1,1024,128]{2,1,0:T(8,128)(2,1)} %bitcast.27, bf16[1,1024,128]{2,1,0:T(8,128)(2,1)S(1)} %bitcast.22, bf16[]{:T(256)} %bitcast.10), kind=kLoop, calls=%fused_computation | loop fusion | flops 2097152 | bytes 2097154 | tf_op jit(solution)/shard_map/add | solution.py:33
  39.1 7.0 %collective-permute-start.4 = (bf16[4,1024,128]{2,1,0:T(8,128)(2,1)}, bf16[4,1024,128]{2,1,0:T(8,128)(2,1)S(1)}, u32[]{:S(2)}, u32[]{:S(2)}) collective-permute-start(bf16[4,1024,128]{2,1,0:T(8,128)(2,1)} %maximum_add_fusion), channel_id=1, source_target_pairs={{0,4},{4,0},{1,5},{5,1},{2,6},{6,2},{3,7},{7,3},{8,12},{12,8},{9,1... | collective-permute-start | bytes 3145736 | tf_op jit(solution)/shard_map/ppermute | solution.py:23
  46.1 0.1 fusion.3.slots
  46.2 2.4 %collective-permute-done.4 = bf16[4,1024,128]{2,1,0:T(8,128)(2,1)S(1)} collective-permute-done((bf16[4,1024,128]{2,1,0:T(8,128)(2,1)}, bf16[4,1024,128]{2,1,0:T(8,128)(2,1)S(1)}, u32[]{:S(2)}, u32[]{:S(2)}) %collective-permute-start.4) | collective-permute-done | bytes 1048608 | tf_op jit(solution)/shard_map/ppermute | solution.py:23
  48.6 0.9 copy-done.2
  49.5 5.2 %shard_map.77 = bf16[4,1024,128]{2,1,0:T(8,128)(2,1)} custom-call(s32[8,16]{1,0:T(8,128)S(1)} %fusion.3.slots, bf16[8,128,128]{2,1,0:T(8,128)(2,1)S(1)} %bitcast.24, bf16[8,128,128]{2,1,0:T(8,128)(2,1)S(1)} %bitcast.23, bf16[8,128,128]{2,1,0:T(8,128)(2,1)} %bitcast.28, bf16[8,128,128]{2,1,0:T(8,128)(2,1)S(1)} %bitcast.21, bf16[8,128,128]{2,1,0:T(8,128)(2,1)S(1)} %bitcast.25, ...), custom_call_target="tpu_custom_call" | custom-call | flops 536870912 | bytes 7340032 | tf_op jit(solution)/shard_map/pallas_call | solution.py:88
  54.8 6.6 %all-to-all-start.1 = ((bf16[4,1024,128]{2,1,0:T(8,128)(2,1)}), bf16[4,1024,128]{2,1,0:T(8,128)(2,1)S(1)}, u32[]{:S(2)}, u32[]{:S(2)}) async-start(bf16[4,1024,128]{2,1,0:T(8,128)(2,1)} %shard_map.77), calls=%async_computation.1 | async-start | bytes 2097152 | tf_op jit(solution)/shard_map/all_to_all | solution.py:164
  61.4 19.2 %all-to-all-done.1.agg = bf16[4,1024,128]{2,1,0:T(8,128)(2,1)S(1)} async-done(((bf16[4,1024,128]{2,1,0:T(8,128)(2,1)}), bf16[4,1024,128]{2,1,0:T(8,128)(2,1)S(1)}, u32[]{:S(2)}, u32[]{:S(2)}) %all-to-all-start.1) | async-done | bytes 1048608 | tf_op jit(solution)/shard_map/all_to_all | solution.py:164
  80.6 3.2 %shard_map.78 = (bf16[1024,128]{1,0:T(8,128)(2,1)}, bf16[128,512]{1,0:T(8,128)(2,1)S(1)}) custom-call(s32[1]{0:T(128)} %bitcast.me, bf16[4,1024,128]{2,1,0:T(8,128)(2,1)S(1)} %all-to-all-done.1.agg, bf16[512,512]{1,0:T(8,128)(2,1)S(1)} %bitcast.18, bf16[1024,512]{1,0:T(8,128)(2,1)S(1)} %copy-done), custom_call_target="tpu_custom_call" | custom-call | tf_op jit(solution)/shard_map/pallas_call | solution.py:136
  83.8 30.0 %all_to_all.25 = bf16[16,8,512]{2,1,0:T(8,128)(2,1)S(1)} all-to-all(bf16[16,8,512]{2,1,0:T(8,128)(2,1)S(1)} %bitcast.26), channel_id=1, replica_groups=mesh['y_lo'=2,'x'=8,'z'=8,'core'=2,'col'=4] {'z','core'}, dimensions={0} | all-to-all | bytes 262144 | tf_op jit(solution)/shard_map/all_to_all | solution.py:164
  113.9 13.9 %all_to_all.26 = bf16[16,8,512]{2,1,0:T(8,128)(2,1)S(1)} all-to-all(bf16[16,8,512]{2,1,0:T(8,128)(2,1)S(1)} %broadcast_in_dim.17), channel_id=1, replica_groups=mesh['y_lo'=2,'x'=8,'z'=8,'core'=2,'col'=4] {'y_lo','x'}, dimensions={0} | all-to-all | bytes 262144 | tf_op jit(solution)/shard_map/all_to_all | solution.py:164
  127.8 13.1 %all_to_all.27 = bf16[16,8,512]{2,1,0:T(8,128)(2,1)S(1)} all-to-all(bf16[16,8,512]{2,1,0:T(8,128)(2,1)S(1)} %broadcast_in_dim.18), channel_id=1, replica_groups=mesh['y_lo'=2,'x'=8,'z'=8,'core'=2,'col'=4] {'z','core'}, dimensions={0} | all-to-all | bytes 262144 | tf_op jit(solution)/shard_map/all_to_all | solution.py:164
  140.9 0.7 bitcast_convert_fusion
  (15 shorter events, 0.1 us)
Async XLA Ops:
  0.6 45.5 %copy-start.4 = (s32[8]{0:T(128)S(1)}, s32[8]{0:T(128)}, u32[]{:S(2)}) copy-start(s32[8]{0:T(128)} %param.9) | copy-start | bytes 100
  0.6 45.5 %copy-start.3 = (s32[8,16]{1,0:T(8,128)S(1)}, s32[8,16]{1,0:T(8,128)}, u32[]{:S(2)}) copy-start(s32[8,16]{1,0:T(8,128)} %param.8) | copy-start | bytes 1540
  2.4 33.4 %all-to-all-start = ((bf16[4,128,512]{2,1,0:T(8,128)(2,1)}), bf16[4,128,512]{2,1,0:T(8,128)(2,1)S(1)}, u32[]{:S(2)}, u32[]{:S(2)}) async-start(bf16[4,128,512]{2,1,0:T(8,128)(2,1)} %broadcast_in_dim.16), calls=%async_computation | async-start | bytes 1048576 | tf_op jit(solution)/shard_map/all_to_all | solution.py:164
  10.5 15.8 %collective-permute-start = (bf16[1024,128]{1,0:T(8,128)(2,1)}, bf16[1024,128]{1,0:T(8,128)(2,1)S(1)}, u32[]{:S(2)}, u32[]{:S(2)}) collective-permute-start(bf16[1024,128]{1,0:T(8,128)(2,1)} %param.6), channel_id=1, source_target_pairs={{0,16},{4,20},{8,24},{12,28},{16,32},{20,36},{24,40},{28,44},{32,4... | collective-permute-start | bytes 786440 | tf_op jit(solution)/shard_map/ppermute | solution.py:19
  18.1 17.6 %collective-permute-start.3 = (bf16[1024,128]{1,0:T(8,128)(2,1)}, bf16[1024,128]{1,0:T(8,128)(2,1)S(1)}, u32[]{:S(2)}, u32[]{:S(2)}) collective-permute-start(bf16[1024,128]{1,0:T(8,128)(2,1)} %param.6), channel_id=1, source_target_pairs={{16,0},{20,4},{24,8},{28,12},{32,16},{36,20},{40,24},{44,28},{48,3... | collective-permute-start | bytes 786440 | tf_op jit(solution)/shard_map/ppermute | solution.py:19
  19.4 17.6 %collective-permute-start.2 = (bf16[1024,128]{1,0:T(8,128)(2,1)}, bf16[1024,128]{1,0:T(8,128)(2,1)S(1)}, u32[]{:S(2)}, u32[]{:S(2)}) collective-permute-start(bf16[1024,128]{1,0:T(8,128)(2,1)} %param.6), channel_id=1, source_target_pairs={{8,0},{12,4},{16,8},{20,12},{24,16},{28,20},{32,24},{36,28},{40,32... | collective-permute-start | bytes 786440 | tf_op jit(solution)/shard_map/ppermute | solution.py:19
  20.7 16.3 %collective-permute-start.1 = (bf16[1024,128]{1,0:T(8,128)(2,1)}, bf16[1024,128]{1,0:T(8,128)(2,1)S(1)}, u32[]{:S(2)}, u32[]{:S(2)}) collective-permute-start(bf16[1024,128]{1,0:T(8,128)(2,1)} %param.6), channel_id=1, source_target_pairs={{0,8},{4,12},{8,16},{12,20},{16,24},{20,28},{24,32},{28,36},{32,40... | collective-permute-start | bytes 786440 | tf_op jit(solution)/shard_map/ppermute | solution.py:19
  35.8 12.8 %copy-start.1 = (bf16[1024,128]{1,0:T(8,128)(2,1)}, bf16[1024,128]{1,0:T(8,128)(2,1)S(1)}, u32[]{:S(2)}) copy-start(bf16[1024,128]{1,0:T(8,128)(2,1)S(1)} %collective-permute-done.3) | copy-start | bytes 786436
  39.1 9.4 %collective-permute-start.4 = (bf16[4,1024,128]{2,1,0:T(8,128)(2,1)}, bf16[4,1024,128]{2,1,0:T(8,128)(2,1)S(1)}, u32[]{:S(2)}, u32[]{:S(2)}) collective-permute-start(bf16[4,1024,128]{2,1,0:T(8,128)(2,1)} %maximum_add_fusion), channel_id=1, source_target_pairs={{0,4},{4,0},{1,5},{5,1},{2,6},{6,2},{3,7},{7,3},{8,12},{12,8},{9,1... | collective-permute-start | bytes 3145736 | tf_op jit(solution)/shard_map/ppermute | solution.py:23
  48.6 1.0 copy-start.2
  49.5 31.0 %copy-start = (bf16[1024,512]{1,0:T(8,128)(2,1)S(1)}, bf16[1024,512]{1,0:T(8,128)(2,1)}, u32[]{:S(2)}) copy-start(bf16[1024,512]{1,0:T(8,128)(2,1)} %cotangent.1) | copy-start | bytes 3145732
  54.8 25.8 %all-to-all-start.1 = ((bf16[4,1024,128]{2,1,0:T(8,128)(2,1)}), bf16[4,1024,128]{2,1,0:T(8,128)(2,1)S(1)}, u32[]{:S(2)}, u32[]{:S(2)}) async-start(bf16[4,1024,128]{2,1,0:T(8,128)(2,1)} %shard_map.77), calls=%async_computation.1 | async-start | bytes 2097152 | tf_op jit(solution)/shard_map/all_to_all | solution.py:164

commit v3 on v2

--- a/solution.py
+++ b/solution.py
@@ -23,16 +23,13 @@
     return lax.ppermute(x, "core", [(0, 1), (1, 0)])
 
 
-def halo(features, weight):
-    whole_weight = spread(weight, "col")
+def halo(features):
     left2, right2 = shifted(features, -4), shifted(features, 4)
     left, right = shifted(features, -2), shifted(features, 2)
     core = lax.axis_index("core")
     edge = jnp.where(core == 0, right2, left2)
-    zero = whole_weight[0, 0, 0] * 0
-    others = swapped(jnp.stack([left, features, right, edge]) + zero)
-    pieces = [(left2, 0), (left, 1), (features, 2), (right, 3), (right2, 4), (others, 5)]
-    return pieces, whole_weight.reshape(-1, weight.shape[1])
+    others = swapped(jnp.stack([left, features, right, edge]))
+    return [(left2, 0), (left, 1), (features, 2), (right, 3), (right2, 4), (others, 5)]
 
 
 def slots_of(tile_cols, tile_count, blocks_here):
@@ -108,7 +105,7 @@
     mine = me[0]
     width = activated.shape[1]
     joined = jnp.concatenate([agg[k] for k in range(agg.shape[0])], axis=1)
-    pre = jnp.dot(joined, weight[...], preferred_element_type=F32)
+    pre = jnp.dot(joined, weight[...].reshape(joined.shape[1], -1), preferred_element_type=F32)
     sigma = 0.5 * jnp.tanh(0.5 * pre) + 0.5
     act[...] = pre * sigma
     activated[...] = act[:, pl.ds(pl.multiple_of(mine * width, width), width)].astype(BF16)
@@ -130,7 +127,7 @@
 
 def dense(agg, weight, cotangent):
     groups, rows, width = agg.shape
-    f_out = weight.shape[1]
+    f_out = weight.shape[-1]
     block = 256
     me = lax.axis_index("col").astype(jnp.int32)[None]
     return pl.pallas_call(
@@ -143,7 +140,7 @@
         in_specs=[
             pl.BlockSpec(memory_space=pltpu.SMEM),
             pl.BlockSpec((groups, block, width), lambda i: (0, i, 0)),
-            pl.BlockSpec((groups * width, f_out), lambda i: (0, 0)),
+            pl.BlockSpec((groups, width, f_out), lambda i: (0, 0, 0)),
             pl.BlockSpec((block, f_out), lambda i: (i, 0)),
         ],
         out_specs=(
@@ -176,8 +173,8 @@
 def shards(features, tile_vals, tile_cols, tile_count, weight, cotangent):
     groups = lax.axis_size("col")
     slots = slots_of(tile_cols, tile_count, tile_vals.shape[0])
-    pieces, whole_weight = halo(features, weight)
-    aggregated = tiles(pieces, slots, tile_vals, groups)
+    whole_weight = lax.all_gather(weight, ("y_lo", "core", "col"))
+    aggregated = tiles(halo(features), slots, tile_vals, groups)
     activated, part = dense(exchanged(aggregated, "col"), whole_weight, cotangent)
     return activated, summed_over_row(part)
 

time: 142 us -> 178 us (1.25)
  waiting for transfers between devices: 31 us -> 81.6 us
  blocking collectives: 57 us -> 43 us
  between operations: 1.47 us -> 14.2 us
  starting transfers between devices: 37.4 us -> 25.6 us
    all_gather x0 -> x1, waiting for transfers between devices: none -> 21.8 us  [shards(): whole_weight = lax.all_gather(weight, ('y_lo', 'core', 'col'))]
    all_to_all x2 -> x1, waiting for transfers between devices: 19.2 us -> 36.2 us  [exchanged(): return lax.all_to_all(x, axes, 0, 0, tiled=True)]
    all_to_all x3, blocking collectives: 57 us -> 43 us  [exchanged(): return lax.all_to_all(x, axes, 0, 0, tiled=True)]
    ppermute x4, waiting for transfers between devices: 9.47 us -> 21.4 us  [shifted(): lax.ppermute(x, ROW, [(i + by, i) for i in range(n) if 0 <= i + by < n])]
    all_to_all x2 -> x1, starting transfers between devices: 14.7 us -> 7.27 us  [exchanged(): return lax.all_to_all(x, axes, 0, 0, tiled=True)]
    ppermute x1, starting transfers between devices: 6.96 us -> 2.3 us  [swapped(): return lax.ppermute(x, 'core', [(0, 1), (1, 0)])]
    add x1 -> x0, other arithmetic: 2.05 us -> none  [halo(): others = swapped(jnp.stack([left, features, right, edge]) + zero)]
  transfers between devices with their start and end apart: 7 -> 7, of which waited for: 3 -> 5; matrix products, arithmetic and copies ran while one was open for 0% -> 1% of each run, Pallas kernels for 0% -> 3%
where the time goes in v3:
time: 178 us; the launch traced here: 177 us
  waiting for transfers between devices  81.6 us (46%)
  blocking collectives  43 us (24%)
  starting transfers between devices  25.6 us (14%)
  between operations  14.2 us (8%)
  Pallas kernels  8.54 us (5%)
  other arithmetic  2.65 us (1%)
    all_to_all x3, blocking collectives, exchanged(): return lax.all_to_all(x, axes, 0, 0, tiled=True)  43 us
    all_to_all x1, waiting for transfers between devices, exchanged(): return lax.all_to_all(x, axes, 0, 0, tiled=True)  36.2 us
    all_gather x1, waiting for transfers between devices, shards(): whole_weight = lax.all_gather(weight, ('y_lo', 'core', 'col'))  21.8 us
    ppermute x4, waiting for transfers between devices, shifted(): lax.ppermute(x, ROW, [(i + by, i) for i in range(n) if 0 <= i + by < n])  21.4 us
    ppermute x4, starting transfers between devices, shifted(): lax.ppermute(x, ROW, [(i + by, i) for i in range(n) if 0 <= i + by < n])  16 us
    all_to_all x1, starting transfers between devices, exchanged(): return lax.all_to_all(x, axes, 0, 0, tiled=True)  7.27 us
    pallas_call x1, Pallas kernels, tiles(): pl.pallas_call(functools.partial(tiles_kernel, starts), out_shape=jax.Sha...  5.28 us
  transfers between devices with their start and end apart: 7, of which 5 were waited for; matrix products, arithmetic and copies ran while one was open for 1% of the time, Pallas kernels for 3%

profile of v3, /device:TPU:1, one launch (start us, length us, event | category | flops | bytes accessed | tf_op | source)
XLA Modules:
  0.0 177.2 jit_solution(3412750067526335590)
XLA Ops:
  7.2 0.0 all-gather.3.cloned.1.call-start
  7.2 0.7 all-gather.3.cloned.1.call-update
  7.9 8.5 %collective-permute-start = (bf16[1024,128]{1,0:T(8,128)(2,1)}, bf16[1024,128]{1,0:T(8,128)(2,1)S(1)}, u32[]{:S(2)}, u32[]{:S(2)}) collective-permute-start(bf16[1024,128]{1,0:T(8,128)(2,1)} %param.6), channel_id=1, source_target_pairs={{0,16},{4,20},{8,24},{12,28},{16,32},{20,36},{24,40},{28,44},{32,4... | collective-permute-start | bytes 786440 | tf_op jit(solution)/shard_map/ppermute | solution.py:19
  16.4 1.3 collective-permute-start.3
  17.7 4.9 %collective-permute-start.1 = (bf16[1024,128]{1,0:T(8,128)(2,1)}, bf16[1024,128]{1,0:T(8,128)(2,1)S(1)}, u32[]{:S(2)}, u32[]{:S(2)}) collective-permute-start(bf16[1024,128]{1,0:T(8,128)(2,1)} %param.6), channel_id=1, source_target_pairs={{0,8},{4,12},{8,16},{12,20},{16,24},{20,28},{24,32},{28,36},{32,40... | collective-permute-start | bytes 786440 | tf_op jit(solution)/shard_map/ppermute | solution.py:19
  22.6 1.3 collective-permute-start.2
  23.9 0.0 collective-permute-done
  23.9 9.0 %collective-permute-done.3 = bf16[1024,128]{1,0:T(8,128)(2,1)S(1)} collective-permute-done((bf16[1024,128]{1,0:T(8,128)(2,1)}, bf16[1024,128]{1,0:T(8,128)(2,1)S(1)}, u32[]{:S(2)}, u32[]{:S(2)}) %collective-permute-start.3) | collective-permute-done | bytes 262176 | tf_op jit(solution)/shard_map/ppermute | solution.py:19
  33.0 0.0 collective-permute-done.1
  33.0 12.4 %collective-permute-done.2 = bf16[1024,128]{1,0:T(8,128)(2,1)S(1)} collective-permute-done((bf16[1024,128]{1,0:T(8,128)(2,1)}, bf16[1024,128]{1,0:T(8,128)(2,1)S(1)}, u32[]{:S(2)}, u32[]{:S(2)}) %collective-permute-start.2) | collective-permute-done | bytes 262176 | tf_op jit(solution)/shard_map/ppermute | solution.py:19
  45.4 1.1 pad_maximum_fusion
  46.5 2.3 %collective-permute-start.4 = (bf16[4,1024,128]{2,1,0:T(8,128)(2,1)S(1)}, bf16[4,1024,128]{2,1,0:T(8,128)(2,1)S(1)}, u32[]{:S(2)}, u32[]{:S(2)}) collective-permute-start(bf16[4,1024,128]{2,1,0:T(8,128)(2,1)S(1)} %pad_maximum_fusion), channel_id=1, source_target_pairs={{0,4},{4,0},{1,5},{5,1},{2,6},{6,2},{3,7},{7,3},{8,12},{12,8},{9,1... | collective-permute-start | bytes 3145736 | tf_op jit(solution)/shard_map/ppermute | solution.py:23
  48.8 0.8 fusion.3.slots
  49.6 1.5 collective-permute-done.4
  51.0 5.3 %shard_map.77 = bf16[4,1024,128]{2,1,0:T(8,128)(2,1)} custom-call(s32[8,16]{1,0:T(8,128)S(1)} %fusion.3.slots, bf16[8,128,128]{2,1,0:T(8,128)(2,1)S(1)} %bitcast.19, bf16[8,128,128]{2,1,0:T(8,128)(2,1)S(1)} %bitcast.22, bf16[8,128,128]{2,1,0:T(8,128)(2,1)} %bitcast.27, bf16[8,128,128]{2,1,0:T(8,128)(2,1)S(1)} %bitcast.24, bf16[8,128,128]{2,1,0:T(8,128)(2,1)S(1)} %bitcast.20, ...), custom_call_target="tpu_custom_call" | custom-call | flops 536870912 | bytes 7340032 | tf_op jit(solution)/shard_map/pallas_call | solution.py:85
  56.3 7.3 %all-to-all-start = ((bf16[4,1024,128]{2,1,0:T(8,128)(2,1)}), bf16[4,1024,128]{2,1,0:T(8,128)(2,1)S(1)}, u32[]{:S(2)}, u32[]{:S(2)}) async-start(bf16[4,1024,128]{2,1,0:T(8,128)(2,1)} %shard_map.77), calls=%async_computation | async-start | bytes 2097152 | tf_op jit(solution)/shard_map/all_to_all | solution.py:161
  63.6 36.2 %all-to-all-done.agg = bf16[4,1024,128]{2,1,0:T(8,128)(2,1)S(1)} async-done(((bf16[4,1024,128]{2,1,0:T(8,128)(2,1)}), bf16[4,1024,128]{2,1,0:T(8,128)(2,1)S(1)}, u32[]{:S(2)}, u32[]{:S(2)}) %all-to-all-start) | async-done | bytes 1048608 | tf_op jit(solution)/shard_map/all_to_all | solution.py:161
  99.8 21.8 %all-gather.3.cloned.1.call-done = bf16[2048,512]{1,0:T(8,128)(2,1)} async-done(((bf16[128,512]{1,0:T(8,128)(2,1)}), bf16[2048,512]{1,0:T(8,128)(2,1)}) %all-gather.3.cloned.1.call-update) | async-done | bytes 2097168 | tf_op jit(solution)/shard_map/all_gather | solution.py:176
  121.7 1.6 copy-done
  123.3 3.3 %shard_map.78 = (bf16[1024,128]{1,0:T(8,128)(2,1)}, bf16[128,512]{1,0:T(8,128)(2,1)S(1)}) custom-call(s32[1]{0:T(128)} %bitcast.me, bf16[4,1024,128]{2,1,0:T(8,128)(2,1)S(1)} %all-to-all-done.agg, bf16[16,128,512]{2,1,0:T(8,128)(2,1)S(1)} %bitcast.17, bf16[1024,512]{1,0:T(8,128)(2,1)S(1)} %copy-done.1), custom_call_target="tpu_custom_call" | custom-call | tf_op jit(solution)/shard_map/pallas_call | solution.py:133
  126.5 18.1 %all_to_all.20 = bf16[16,8,512]{2,1,0:T(8,128)(2,1)S(1)} all-to-all(bf16[16,8,512]{2,1,0:T(8,128)(2,1)S(1)} %bitcast.25), channel_id=1, replica_groups=mesh['y_lo'=2,'x'=8,'z'=8,'core'=2,'col'=4] {'z','core'}, dimensions={0} | all-to-all | bytes 262144 | tf_op jit(solution)/shard_map/all_to_all | solution.py:161
  144.7 11.8 %all_to_all.21 = bf16[16,8,512]{2,1,0:T(8,128)(2,1)S(1)} all-to-all(bf16[16,8,512]{2,1,0:T(8,128)(2,1)S(1)} %broadcast_in_dim.14), channel_id=1, replica_groups=mesh['y_lo'=2,'x'=8,'z'=8,'core'=2,'col'=4] {'y_lo','x'}, dimensions={0} | all-to-all | bytes 262144 | tf_op jit(solution)/shard_map/all_to_all | solution.py:161
  156.6 13.1 %all_to_all.22 = bf16[16,8,512]{2,1,0:T(8,128)(2,1)S(1)} all-to-all(bf16[16,8,512]{2,1,0:T(8,128)(2,1)S(1)} %broadcast_in_dim.26), channel_id=1, replica_groups=mesh['y_lo'=2,'x'=8,'z'=8,'core'=2,'col'=4] {'z','core'}, dimensions={0} | all-to-all | bytes 262144 | tf_op jit(solution)/shard_map/all_to_all | solution.py:161
  169.6 0.7 bitcast_convert_fusion
  (8 shorter events, 0.1 us)
Async XLA Ops:
  7.2 114.5 %all-gather.3.cloned.1.call-start = ((), (), s32[]{:S(2)}) async-start(), calls=%async_computation.4 | async-start | bytes 2228224 | tf_op jit(solution)/shard_map/all_gather | solution.py:176
  7.9 16.0 %collective-permute-start = (bf16[1024,128]{1,0:T(8,128)(2,1)}, bf16[1024,128]{1,0:T(8,128)(2,1)S(1)}, u32[]{:S(2)}, u32[]{:S(2)}) collective-permute-start(bf16[1024,128]{1,0:T(8,128)(2,1)} %param.6), channel_id=1, source_target_pairs={{0,16},{4,20},{8,24},{12,28},{16,32},{20,36},{24,40},{28,44},{32,4... | collective-permute-start | bytes 786440 | tf_op jit(solution)/shard_map/ppermute | solution.py:19
  16.4 16.5 %collective-permute-start.3 = (bf16[1024,128]{1,0:T(8,128)(2,1)}, bf16[1024,128]{1,0:T(8,128)(2,1)S(1)}, u32[]{:S(2)}, u32[]{:S(2)}) collective-permute-start(bf16[1024,128]{1,0:T(8,128)(2,1)} %param.6), channel_id=1, source_target_pairs={{16,0},{20,4},{24,8},{28,12},{32,16},{36,20},{40,24},{44,28},{48,3... | collective-permute-start | bytes 786440 | tf_op jit(solution)/shard_map/ppermute | solution.py:19
  17.7 15.3 %collective-permute-start.1 = (bf16[1024,128]{1,0:T(8,128)(2,1)}, bf16[1024,128]{1,0:T(8,128)(2,1)S(1)}, u32[]{:S(2)}, u32[]{:S(2)}) collective-permute-start(bf16[1024,128]{1,0:T(8,128)(2,1)} %param.6), channel_id=1, source_target_pairs={{0,8},{4,12},{8,16},{12,20},{16,24},{20,28},{24,32},{28,36},{32,40... | collective-permute-start | bytes 786440 | tf_op jit(solution)/shard_map/ppermute | solution.py:19
  22.6 22.8 %collective-permute-start.2 = (bf16[1024,128]{1,0:T(8,128)(2,1)}, bf16[1024,128]{1,0:T(8,128)(2,1)S(1)}, u32[]{:S(2)}, u32[]{:S(2)}) collective-permute-start(bf16[1024,128]{1,0:T(8,128)(2,1)} %param.6), channel_id=1, source_target_pairs={{8,0},{12,4},{16,8},{20,12},{24,16},{28,20},{32,24},{36,28},{40,32... | collective-permute-start | bytes 786440 | tf_op jit(solution)/shard_map/ppermute | solution.py:19
  46.5 4.6 %collective-permute-start.4 = (bf16[4,1024,128]{2,1,0:T(8,128)(2,1)S(1)}, bf16[4,1024,128]{2,1,0:T(8,128)(2,1)S(1)}, u32[]{:S(2)}, u32[]{:S(2)}) collective-permute-start(bf16[4,1024,128]{2,1,0:T(8,128)(2,1)S(1)} %pad_maximum_fusion), channel_id=1, source_target_pairs={{0,4},{4,0},{1,5},{5,1},{2,6},{6,2},{3,7},{7,3},{8,12},{12,8},{9,1... | collective-permute-start | bytes 3145736 | tf_op jit(solution)/shard_map/ppermute | solution.py:23
  51.0 70.6 %copy-start.1 = (bf16[1024,512]{1,0:T(8,128)(2,1)S(1)}, bf16[1024,512]{1,0:T(8,128)(2,1)}, u32[]{:S(2)}) copy-start(bf16[1024,512]{1,0:T(8,128)(2,1)} %cotangent.1) | copy-start | bytes 3145732
  56.3 43.5 %all-to-all-start = ((bf16[4,1024,128]{2,1,0:T(8,128)(2,1)}), bf16[4,1024,128]{2,1,0:T(8,128)(2,1)S(1)}, u32[]{:S(2)}, u32[]{:S(2)}) async-start(bf16[4,1024,128]{2,1,0:T(8,128)(2,1)} %shard_map.77), calls=%async_computation | async-start | bytes 2097152 | tf_op jit(solution)/shard_map/all_to_all | solution.py:161
  121.7 1.6 copy-start
Sparse Core Ops, SparseCore 0:
  10.7 110.9 all-gather.2

commit v4 on v2

--- a/solution.py
+++ b/solution.py
@@ -14,24 +14,24 @@
 BF16 = jnp.bfloat16
 
 
-def shifted(x, by):
-    n = lax.axis_size(ROW)
-    return lax.ppermute(x, ROW, [(i + by, i) for i in range(n) if 0 <= i + by < n])
-
-
 def swapped(x):
     return lax.ppermute(x, "core", [(0, 1), (1, 0)])
 
 
+def passed_on(x):
+    n = lax.axis_size(ROW)
+    up = [(i, i + 2) for i in range(0, n - 2, 2)]
+    down = [(i, i - 2) for i in range(3, n, 2)]
+    return lax.ppermute(x, ROW, up + down)
+
+
 def halo(features, weight):
+    other = swapped(features)
+    one = passed_on(jnp.stack([features, other]))
+    two = passed_on(one)
     whole_weight = spread(weight, "col")
-    left2, right2 = shifted(features, -4), shifted(features, 4)
-    left, right = shifted(features, -2), shifted(features, 2)
-    core = lax.axis_index("core")
-    edge = jnp.where(core == 0, right2, left2)
-    zero = whole_weight[0, 0, 0] * 0
-    others = swapped(jnp.stack([left, features, right, edge]) + zero)
-    pieces = [(left2, 0), (left, 1), (features, 2), (right, 3), (right2, 4), (others, 5)]
+    last = swapped(two[1] + whole_weight[0, 0, 0] * 0)
+    pieces = [(features, 0), (other, 1), (one, 2), (two, 4), (swapped(one), 6), (last, 8)]
     return pieces, whole_weight.reshape(-1, weight.shape[1])
 
 
@@ -39,9 +39,14 @@
     device = lax.axis_index(ROW)
     source = tile_cols // blocks_here
     chip = source // 2 - device // 2
-    same = source % 2 == device % 2
-    other = jnp.where(jnp.abs(chip) == 2, 8, chip + 6)
-    group = jnp.where(same, chip + 2, other)
+    core = device % 2
+    same = source % 2 == core
+    second = jnp.where(same, 0, 1)
+    own_side = (chip < 0) == (core == 0)
+    one = jnp.where(own_side, 2 + second, 7 - second)
+    two = jnp.where(own_side, 4 + second, 8)
+    distance = jnp.abs(chip)
+    group = jnp.where(distance == 0, second, jnp.where(distance == 1, one, two))
     slot = group * blocks_here + tile_cols % blocks_here
     keep = jnp.arange(tile_cols.shape[1], dtype=jnp.int32)[None, :] < tile_count[:, None]
     return jnp.where(keep, slot, 9 * blocks_here)
@@ -81,6 +86,7 @@
     blocks, count, tile, _ = tile_vals.shape
     cols = pieces[0][0].shape[-1]
     arrays = [x.reshape(-1, tile, cols) for x, _ in pieces]
+    arrays[0] = pltpu.with_memory_space_constraint(arrays[0], pltpu.HBM)
     arrays[2] = pltpu.with_memory_space_constraint(arrays[2], pltpu.HBM)
     starts = [group * blocks for _, group in pieces]
     anywhere = pl.BlockSpec(memory_space=pl.ANY)

time: 142 us -> 134 us (0.944)
  starting transfers between devices: 37.4 us -> 32.6 us
  waiting for transfers between devices: 31 us -> 28.2 us
    ppermute x1 -> x3, starting transfers between devices: 6.96 us -> 23 us  [swapped(): return lax.ppermute(x, 'core', [(0, 1), (1, 0)])]
    ppermute x4 -> x2, starting transfers between devices: 15.8 us -> 2.57 us  [passed_on(): return lax.ppermute(x, ROW, up + down)]
    all_to_all x2, starting transfers between devices: 14.7 us -> 7 us  [exchanged(): return lax.all_to_all(x, axes, 0, 0, tiled=True)]
    ppermute x4 -> x2, waiting for transfers between devices: 9.47 us -> 3.54 us  [passed_on(): return lax.ppermute(x, ROW, up + down)]
    all_to_all x2, waiting for transfers between devices: 19.2 us -> 22.9 us  [exchanged(): return lax.all_to_all(x, axes, 0, 0, tiled=True)]
    add x1, other arithmetic: 2.05 us -> 0.02 us  [halo(): last = swapped(two[1] + whole_weight[0, 0, 0] * 0)]
  transfers between devices with their start and end apart: 7 -> 7, of which waited for: 3 -> 6; matrix products, arithmetic and copies ran while one was open for 0% -> 2% of each run, Pallas kernels for 0% -> 0%
where the time goes in v4:
time: 134 us; the launch traced here: 133 us
  blocking collectives  57.8 us (43%)
  starting transfers between devices  32.6 us (24%)
  waiting for transfers between devices  28.2 us (21%)
  Pallas kernels  8.6 us (6%)
  other arithmetic  2.56 us (2%)
  local copies, waits for them, and re-layouts  2.28 us (2%)
  between operations  1.41 us (1%)
    all_to_all x3, blocking collectives, exchanged(): return lax.all_to_all(x, axes, 0, 0, tiled=True)  57.8 us
    ppermute x3, starting transfers between devices, swapped(): return lax.ppermute(x, 'core', [(0, 1), (1, 0)])  23 us
    all_to_all x2, waiting for transfers between devices, exchanged(): return lax.all_to_all(x, axes, 0, 0, tiled=True)  22.9 us
    all_to_all x2, starting transfers between devices, exchanged(): return lax.all_to_all(x, axes, 0, 0, tiled=True)  7 us
    pallas_call x1, Pallas kernels, tiles(): pl.pallas_call(functools.partial(tiles_kernel, starts), out_shape=jax.Sha...  5.35 us
    ppermute x2, waiting for transfers between devices, passed_on(): return lax.ppermute(x, ROW, up + down)  3.54 us
    pallas_call x1, Pallas kernels, dense(): pl.pallas_call(dense_kernel, out_shape=(jax.ShapeDtypeStruct((rows, f_out...  3.24 us
  transfers between devices with their start and end apart: 7, of which 6 were waited for; matrix products, arithmetic and copies ran while one was open for 2% of the time, Pallas kernels for 0%

profile of v4, /device:TPU:1, one launch (start us, length us, event | category | flops | bytes accessed | tf_op | source)
XLA Modules:
  0.0 133.4 jit_solution(10898490548608366771)
XLA Ops:
  0.6 16.1 %collective-permute-start = (bf16[1024,128]{1,0:T(8,128)(2,1)}, bf16[1024,128]{1,0:T(8,128)(2,1)S(1)}, u32[]{:S(2)}, u32[]{:S(2)}) collective-permute-start(bf16[1024,128]{1,0:T(8,128)(2,1)} %param.6), channel_id=1, source_target_pairs={{0,4},{4,0},{1,5},{5,1},{2,6},{6,2},{3,7},{7,3},{8,12},{12,8},{9,1... | collective-permute-start | bytes 786440 | tf_op jit(solution)/shard_map/ppermute | solution.py:18
  16.7 1.4 %collective-permute-done = bf16[1024,128]{1,0:T(8,128)(2,1)S(1)} collective-permute-done((bf16[1024,128]{1,0:T(8,128)(2,1)}, bf16[1024,128]{1,0:T(8,128)(2,1)S(1)}, u32[]{:S(2)}, u32[]{:S(2)}) %collective-permute-start) | collective-permute-done | bytes 262176 | tf_op jit(solution)/shard_map/ppermute | solution.py:18
  18.1 1.0 pad_maximum_fusion
  19.1 1.3 collective-permute-start.1
  20.4 1.7 %broadcast_in_dim.20 = bf16[4,128,512]{2,1,0:T(8,128)(2,1)} broadcast(bf16[128,512]{1,0:T(8,128)(2,1)} %param.10), dimensions={1,2} | broadcast | bytes 655360 | tf_op jit(solution)/shard_map/broadcast_in_dim | solution.py:166
  22.1 3.5 %all-to-all-start = ((bf16[4,128,512]{2,1,0:T(8,128)(2,1)}), bf16[4,128,512]{2,1,0:T(8,128)(2,1)S(1)}, u32[]{:S(2)}, u32[]{:S(2)}) async-start(bf16[4,128,512]{2,1,0:T(8,128)(2,1)} %broadcast_in_dim.20), calls=%async_computation | async-start | bytes 1048576 | tf_op jit(solution)/shard_map/all_to_all | solution.py:170
  25.6 3.4 %collective-permute-done.1 = bf16[2,1024,128]{2,1,0:T(8,128)(2,1)S(1)} collective-permute-done((bf16[2,1024,128]{2,1,0:T(8,128)(2,1)S(1)}, bf16[2,1024,128]{2,1,0:T(8,128)(2,1)S(1)}, u32[]{:S(2)}, u32[]{:S(2)}) %collective-permute-start.1) | collective-permute-done | bytes 524320 | tf_op jit(solution)/shard_map/ppermute | solution.py:25
  29.0 1.3 collective-permute-start.2
  30.3 3.5 %collective-permute-start.3 = (bf16[2,1024,128]{2,1,0:T(8,128)(2,1)S(1)}, bf16[2,1024,128]{2,1,0:T(8,128)(2,1)S(1)}, u32[]{:S(2)}, u32[]{:S(2)}) collective-permute-start(bf16[2,1024,128]{2,1,0:T(8,128)(2,1)S(1)} %collective-permute-done.1), channel_id=1, source_target_pairs={{0,4},{4,0},{1,5},{5,1},{2,6},{6,2},{3,7},{7,3},{8,12},{12,8},{9,1... | collective-permute-start | bytes 1572872 | tf_op jit(solution)/shard_map/ppermute | solution.py:18
  33.7 3.9 %all-to-all-done = bf16[4,128,512]{2,1,0:T(8,128)(2,1)S(1)} async-done(((bf16[4,128,512]{2,1,0:T(8,128)(2,1)}), bf16[4,128,512]{2,1,0:T(8,128)(2,1)S(1)}, u32[]{:S(2)}, u32[]{:S(2)}) %all-to-all-start) | async-done | bytes 524320 | tf_op jit(solution)/shard_map/all_to_all | solution.py:170
  37.6 0.5 slice.9
  38.8 0.1 collective-permute-done.2
  38.9 3.5 %collective-permute-start.4 = (bf16[1024,128]{1,0:T(8,128)(2,1)S(1)}, bf16[1024,128]{1,0:T(8,128)(2,1)S(1)}, u32[]{:S(2)}, u32[]{:S(2)}) collective-permute-start(bf16[1024,128]{1,0:T(8,128)(2,1)S(1)} %fusion), channel_id=1, source_target_pairs={{0,4},{4,0},{1,5},{5,1},{2,6},{6,2},{3,7},{7,3},{8,12},{12,8},{9,1... | collective-permute-start | bytes 786440 | tf_op jit(solution)/shard_map/ppermute | solution.py:18
  42.4 0.8 fusion.4.slots
  43.2 0.0 collective-permute-done.3
  43.2 0.3 collective-permute-done.4
  43.5 5.4 %shard_map.77 = bf16[4,1024,128]{2,1,0:T(8,128)(2,1)} custom-call(s32[8,16]{1,0:T(8,128)S(1)} %fusion.4.slots, bf16[8,128,128]{2,1,0:T(8,128)(2,1)} %bitcast.25, bf16[8,128,128]{2,1,0:T(8,128)(2,1)S(1)} %bitcast.20, bf16[16,128,128]{2,1,0:T(8,128)(2,1)} %bitcast.26, bf16[16,128,128]{2,1,0:T(8,128)(2,1)S(1)} %bitcast.18, bf16[16,128,128]{2,1,0:T(8,128)(2,1)S(1)} %bitcast.21, ...), custom_call_target="tpu_custom_call" | custom-call | flops 536870912 | bytes 7340032 | tf_op jit(solution)/shard_map/pallas_call | solution.py:94
  48.9 3.5 %all-to-all-start.1 = ((bf16[4,1024,128]{2,1,0:T(8,128)(2,1)}), bf16[4,1024,128]{2,1,0:T(8,128)(2,1)S(1)}, u32[]{:S(2)}, u32[]{:S(2)}) async-start(bf16[4,1024,128]{2,1,0:T(8,128)(2,1)} %shard_map.77), calls=%async_computation.1 | async-start | bytes 2097152 | tf_op jit(solution)/shard_map/all_to_all | solution.py:170
  52.4 19.1 %all-to-all-done.1.agg = bf16[4,1024,128]{2,1,0:T(8,128)(2,1)S(1)} async-done(((bf16[4,1024,128]{2,1,0:T(8,128)(2,1)}), bf16[4,1024,128]{2,1,0:T(8,128)(2,1)S(1)}, u32[]{:S(2)}, u32[]{:S(2)}) %all-to-all-start.1) | async-done | bytes 1048608 | tf_op jit(solution)/shard_map/all_to_all | solution.py:170
  71.5 3.2 %shard_map.78 = (bf16[1024,128]{1,0:T(8,128)(2,1)}, bf16[128,512]{1,0:T(8,128)(2,1)S(1)}) custom-call(s32[1]{0:T(128)} %bitcast.me, bf16[4,1024,128]{2,1,0:T(8,128)(2,1)S(1)} %all-to-all-done.1.agg, bf16[512,512]{1,0:T(8,128)(2,1)S(1)} %bitcast.17, bf16[1024,512]{1,0:T(8,128)(2,1)S(1)} %copy-done), custom_call_target="tpu_custom_call" | custom-call | tf_op jit(solution)/shard_map/pallas_call | solution.py:142
  74.7 31.2 %all_to_all.25 = bf16[16,8,512]{2,1,0:T(8,128)(2,1)S(1)} all-to-all(bf16[16,8,512]{2,1,0:T(8,128)(2,1)S(1)} %bitcast.23), channel_id=1, replica_groups=mesh['y_lo'=2,'x'=8,'z'=8,'core'=2,'col'=4] {'z','core'}, dimensions={0} | all-to-all | bytes 262144 | tf_op jit(solution)/shard_map/all_to_all | solution.py:170
  106.0 13.5 %all_to_all.26 = bf16[16,8,512]{2,1,0:T(8,128)(2,1)S(1)} all-to-all(bf16[16,8,512]{2,1,0:T(8,128)(2,1)S(1)} %broadcast_in_dim.21), channel_id=1, replica_groups=mesh['y_lo'=2,'x'=8,'z'=8,'core'=2,'col'=4] {'y_lo','x'}, dimensions={0} | all-to-all | bytes 262144 | tf_op jit(solution)/shard_map/all_to_all | solution.py:170
  119.6 13.1 %all_to_all.27 = bf16[16,8,512]{2,1,0:T(8,128)(2,1)S(1)} all-to-all(bf16[16,8,512]{2,1,0:T(8,128)(2,1)S(1)} %broadcast_in_dim.22), channel_id=1, replica_groups=mesh['y_lo'=2,'x'=8,'z'=8,'core'=2,'col'=4] {'z','core'}, dimensions={0} | all-to-all | bytes 262144 | tf_op jit(solution)/shard_map/all_to_all | solution.py:170
  132.6 0.7 bitcast_convert_fusion
  (9 shorter events, 0.1 us)
Async XLA Ops:
  0.6 17.4 %collective-permute-start = (bf16[1024,128]{1,0:T(8,128)(2,1)}, bf16[1024,128]{1,0:T(8,128)(2,1)S(1)}, u32[]{:S(2)}, u32[]{:S(2)}) collective-permute-start(bf16[1024,128]{1,0:T(8,128)(2,1)} %param.6), channel_id=1, source_target_pairs={{0,4},{4,0},{1,5},{5,1},{2,6},{6,2},{3,7},{7,3},{8,12},{12,8},{9,1... | collective-permute-start | bytes 786440 | tf_op jit(solution)/shard_map/ppermute | solution.py:18
  19.1 9.9 %collective-permute-start.1 = (bf16[2,1024,128]{2,1,0:T(8,128)(2,1)S(1)}, bf16[2,1024,128]{2,1,0:T(8,128)(2,1)S(1)}, u32[]{:S(2)}, u32[]{:S(2)}) collective-permute-start(bf16[2,1024,128]{2,1,0:T(8,128)(2,1)S(1)} %pad_maximum_fusion), channel_id=1, source_target_pairs={{0,8},{8,16},{16,24},{24,32},{32,40},{40,48},{48,56},{56,64},{64,7... | collective-permute-start | bytes 1572872 | tf_op jit(solution)/shard_map/ppermute | solution.py:25
  22.1 15.5 %all-to-all-start = ((bf16[4,128,512]{2,1,0:T(8,128)(2,1)}), bf16[4,128,512]{2,1,0:T(8,128)(2,1)S(1)}, u32[]{:S(2)}, u32[]{:S(2)}) async-start(bf16[4,128,512]{2,1,0:T(8,128)(2,1)} %broadcast_in_dim.20), calls=%async_computation | async-start | bytes 1048576 | tf_op jit(solution)/shard_map/all_to_all | solution.py:170
  29.0 14.5 %copy-start.1 = (bf16[2,1024,128]{2,1,0:T(8,128)(2,1)}, bf16[2,1024,128]{2,1,0:T(8,128)(2,1)S(1)}, u32[]{:S(2)}) copy-start(bf16[2,1024,128]{2,1,0:T(8,128)(2,1)S(1)} %collective-permute-done.1) | copy-start | bytes 1572868
  29.0 9.9 %collective-permute-start.2 = (bf16[2,1024,128]{2,1,0:T(8,128)(2,1)S(1)}, bf16[2,1024,128]{2,1,0:T(8,128)(2,1)S(1)}, u32[]{:S(2)}, u32[]{:S(2)}) collective-permute-start(bf16[2,1024,128]{2,1,0:T(8,128)(2,1)S(1)} %collective-permute-done.1), channel_id=1, source_target_pairs={{0,8},{8,16},{16,24},{24,32},{32,40},{40,48},{48,56},{56,64},{64,7... | collective-permute-start | bytes 1572872 | tf_op jit(solution)/shard_map/ppermute | solution.py:25
  30.3 12.9 %collective-permute-start.3 = (bf16[2,1024,128]{2,1,0:T(8,128)(2,1)S(1)}, bf16[2,1024,128]{2,1,0:T(8,128)(2,1)S(1)}, u32[]{:S(2)}, u32[]{:S(2)}) collective-permute-start(bf16[2,1024,128]{2,1,0:T(8,128)(2,1)S(1)} %collective-permute-done.1), channel_id=1, source_target_pairs={{0,4},{4,0},{1,5},{5,1},{2,6},{6,2},{3,7},{7,3},{8,12},{12,8},{9,1... | collective-permute-start | bytes 1572872 | tf_op jit(solution)/shard_map/ppermute | solution.py:18
  38.9 4.6 %collective-permute-start.4 = (bf16[1024,128]{1,0:T(8,128)(2,1)S(1)}, bf16[1024,128]{1,0:T(8,128)(2,1)S(1)}, u32[]{:S(2)}, u32[]{:S(2)}) collective-permute-start(bf16[1024,128]{1,0:T(8,128)(2,1)S(1)} %fusion), channel_id=1, source_target_pairs={{0,4},{4,0},{1,5},{5,1},{2,6},{6,2},{3,7},{7,3},{8,12},{12,8},{9,1... | collective-permute-start | bytes 786440 | tf_op jit(solution)/shard_map/ppermute | solution.py:18
  43.5 28.0 %copy-start = (bf16[1024,512]{1,0:T(8,128)(2,1)S(1)}, bf16[1024,512]{1,0:T(8,128)(2,1)}, u32[]{:S(2)}) copy-start(bf16[1024,512]{1,0:T(8,128)(2,1)} %cotangent.1) | copy-start | bytes 3145732
  48.9 22.6 %all-to-all-start.1 = ((bf16[4,1024,128]{2,1,0:T(8,128)(2,1)}), bf16[4,1024,128]{2,1,0:T(8,128)(2,1)S(1)}, u32[]{:S(2)}, u32[]{:S(2)}) async-start(bf16[4,1024,128]{2,1,0:T(8,128)(2,1)} %shard_map.77), calls=%async_computation.1 | async-start | bytes 2097152 | tf_op jit(solution)/shard_map/all_to_all | solution.py:170

commit v5 on v4

--- a/solution.py
+++ b/solution.py
@@ -25,14 +25,16 @@
     return lax.ppermute(x, ROW, up + down)
 
 
-def halo(features, weight):
+def halo(features):
+    one = passed_on(features)
     other = swapped(features)
-    one = passed_on(jnp.stack([features, other]))
+    one_other = passed_on(other)
     two = passed_on(one)
-    whole_weight = spread(weight, "col")
-    last = swapped(two[1] + whole_weight[0, 0, 0] * 0)
-    pieces = [(features, 0), (other, 1), (one, 2), (two, 4), (swapped(one), 6), (last, 8)]
-    return pieces, whole_weight.reshape(-1, weight.shape[1])
+    two_other = passed_on(one_other)
+    across = swapped(jnp.stack([one, one_other]))
+    last = swapped(two_other)
+    arrays = [features, other, one, one_other, two, two_other, across, last]
+    return list(zip(arrays, [0, 1, 2, 3, 4, 5, 6, 8]))
 
 
 def slots_of(tile_cols, tile_count, blocks_here):
@@ -54,7 +56,7 @@
 
 def tiles_kernel(starts, slots, *refs):
     pieces = refs[: len(starts)]
-    vals_hbm, out, window, vals, piece_sems, vals_sems = refs[len(starts) :]
+    vals_hbm, _, out, window, vals, piece_sems, vals_sems = refs[len(starts) :]
     blocks, count, tile, cols = vals.shape[0], vals.shape[1], vals.shape[2], window.shape[2]
     copies = [
         pltpu.make_async_copy(piece, window.at[pl.ds(start, piece.shape[0])], piece_sems.at[i])
@@ -82,19 +84,20 @@
             out[k, pl.ds(b * tile, tile), :] = done
 
 
-def tiles(pieces, slots, tile_vals, times):
+def tiles(pieces, slots, tile_vals, weight):
+    times = weight.shape[0]
     blocks, count, tile, _ = tile_vals.shape
     cols = pieces[0][0].shape[-1]
     arrays = [x.reshape(-1, tile, cols) for x, _ in pieces]
     arrays[0] = pltpu.with_memory_space_constraint(arrays[0], pltpu.HBM)
-    arrays[2] = pltpu.with_memory_space_constraint(arrays[2], pltpu.HBM)
+    arrays[7] = pltpu.with_memory_space_constraint(arrays[7], pltpu.HBM)
     starts = [group * blocks for _, group in pieces]
     anywhere = pl.BlockSpec(memory_space=pl.ANY)
     hbm = pl.BlockSpec(memory_space=pltpu.HBM)
     return pl.pallas_call(
         functools.partial(tiles_kernel, starts),
         out_shape=jax.ShapeDtypeStruct((times, blocks * tile, cols), BF16),
-        in_specs=[pl.BlockSpec(memory_space=pltpu.SMEM)] + [anywhere] * len(arrays) + [hbm],
+        in_specs=[pl.BlockSpec(memory_space=pltpu.SMEM)] + [anywhere] * len(arrays) + [hbm, anywhere],
         out_specs=pl.BlockSpec(memory_space=pltpu.VMEM),
         scratch_shapes=[
             pltpu.VMEM((9 * blocks + 1, tile, cols), BF16),
@@ -106,7 +109,7 @@
         cost_estimate=pl.CostEstimate(
             flops=2 * blocks * count * tile * tile * cols, bytes_accessed=7 << 20, transcendentals=0
         ),
-    )(slots, *arrays, pltpu.with_memory_space_constraint(tile_vals, pltpu.HBM))
+    )(slots, *arrays, pltpu.with_memory_space_constraint(tile_vals, pltpu.HBM), weight)
 
 
 def dense_kernel(me, agg, weight, cotangent, activated, grad, act, total):
@@ -180,10 +183,10 @@
 
 
 def shards(features, tile_vals, tile_cols, tile_count, weight, cotangent):
-    groups = lax.axis_size("col")
     slots = slots_of(tile_cols, tile_count, tile_vals.shape[0])
-    pieces, whole_weight = halo(features, weight)
-    aggregated = tiles(pieces, slots, tile_vals, groups)
+    whole_weight = spread(weight, "col")
+    aggregated = tiles(halo(features), slots, tile_vals, whole_weight)
+    whole_weight = whole_weight.reshape(-1, weight.shape[1])
     activated, part = dense(exchanged(aggregated, "col"), whole_weight, cotangent)
     return activated, summed_over_row(part)
 

time: 134 us -> 134 us (level)
  starting transfers between devices: 32.6 us -> 42.7 us
  waiting for transfers between devices: 28.2 us -> 22.4 us
  blocking collectives: 57.8 us -> 54 us
    ppermute x3, starting transfers between devices: 23 us -> 27.1 us  [swapped(): return lax.ppermute(x, 'core', [(0, 1), (1, 0)])]
    all_to_all x2, waiting for transfers between devices: 22.9 us -> 19 us  [exchanged(): return lax.all_to_all(x, axes, 0, 0, tiled=True)]
    all_to_all x3, blocking collectives: 57.8 us -> 54 us  [exchanged(): return lax.all_to_all(x, axes, 0, 0, tiled=True)]
    all_to_all x2, starting transfers between devices: 7 us -> 10.4 us  [exchanged(): return lax.all_to_all(x, axes, 0, 0, tiled=True)]
    ppermute x2 -> x4, starting transfers between devices: 2.57 us -> 5.16 us  [passed_on(): return lax.ppermute(x, ROW, up + down)]
    ppermute x2 -> x4, waiting for transfers between devices: 3.54 us -> 2.12 us  [passed_on(): return lax.ppermute(x, ROW, up + down)]
  transfers between devices with their start and end apart: 7 -> 9, of which waited for: 6 -> 5; matrix products, arithmetic and copies ran while one was open for 2% -> 2% of each run, Pallas kernels for 0% -> 0%
where the time goes in v5:
time: 134 us; the launch traced here: 133 us
  blocking collectives  54 us (40%)
  starting transfers between devices  42.7 us (32%)
  waiting for transfers between devices  22.4 us (17%)
  Pallas kernels  9.35 us (7%)
  local copies, waits for them, and re-layouts  2.47 us (2%)
  other arithmetic  1.59 us (1%)
    all_to_all x3, blocking collectives, exchanged(): return lax.all_to_all(x, axes, 0, 0, tiled=True)  54 us
    ppermute x3, starting transfers between devices, swapped(): return lax.ppermute(x, 'core', [(0, 1), (1, 0)])  27.1 us
    all_to_all x2, waiting for transfers between devices, exchanged(): return lax.all_to_all(x, axes, 0, 0, tiled=True)  19 us
    all_to_all x2, starting transfers between devices, exchanged(): return lax.all_to_all(x, axes, 0, 0, tiled=True)  10.4 us
    pallas_call x1, Pallas kernels, tiles(): pl.pallas_call(functools.partial(tiles_kernel, starts), out_shape=jax.Sha...  6.11 us
    ppermute x4, starting transfers between devices, passed_on(): return lax.ppermute(x, ROW, up + down)  5.16 us
    pallas_call x1, Pallas kernels, dense(): pl.pallas_call(dense_kernel, out_shape=(jax.ShapeDtypeStruct((rows, f_out...  3.24 us
  transfers between devices with their start and end apart: 9, of which 5 were waited for; matrix products, arithmetic and copies ran while one was open for 2% of the time, Pallas kernels for 0%

profile of v5, /device:TPU:1, one launch (start us, length us, event | category | flops | bytes accessed | tf_op | source)
XLA Modules:
  0.0 133.3 jit_solution(10012376685460464262)
XLA Ops:
  0.6 16.1 %collective-permute-start = (bf16[1024,128]{1,0:T(8,128)(2,1)}, bf16[1024,128]{1,0:T(8,128)(2,1)S(1)}, u32[]{:S(2)}, u32[]{:S(2)}) collective-permute-start(bf16[1024,128]{1,0:T(8,128)(2,1)} %param.6), channel_id=1, source_target_pairs={{0,4},{4,0},{1,5},{5,1},{2,6},{6,2},{3,7},{7,3},{8,12},{12,8},{9,1... | collective-permute-start | bytes 786440 | tf_op jit(solution)/shard_map/ppermute | solution.py:18
  16.7 1.4 %collective-permute-done = bf16[1024,128]{1,0:T(8,128)(2,1)S(1)} collective-permute-done((bf16[1024,128]{1,0:T(8,128)(2,1)}, bf16[1024,128]{1,0:T(8,128)(2,1)S(1)}, u32[]{:S(2)}, u32[]{:S(2)}) %collective-permute-start) | collective-permute-done | bytes 262176 | tf_op jit(solution)/shard_map/ppermute | solution.py:18
  18.1 1.3 collective-permute-start.2
  19.3 1.3 collective-permute-start.1
  20.6 1.7 %broadcast_in_dim.20 = bf16[4,128,512]{2,1,0:T(8,128)(2,1)} broadcast(bf16[128,512]{1,0:T(8,128)(2,1)} %param.10), dimensions={1,2} | broadcast | bytes 655360 | tf_op jit(solution)/shard_map/broadcast_in_dim | solution.py:169
  22.4 3.5 %all-to-all-start = ((bf16[4,128,512]{2,1,0:T(8,128)(2,1)}), bf16[4,128,512]{2,1,0:T(8,128)(2,1)S(1)}, u32[]{:S(2)}, u32[]{:S(2)}) async-start(bf16[4,128,512]{2,1,0:T(8,128)(2,1)} %broadcast_in_dim.20), calls=%async_computation | async-start | bytes 1048576 | tf_op jit(solution)/shard_map/all_to_all | solution.py:173
  25.9 1.3 collective-permute-start.4
  27.2 0.8 collective-permute-done.1
  28.0 0.1 pad_maximum_fusion
  28.0 4.6 %collective-permute-start.5 = (bf16[2,1024,128]{2,1,0:T(8,128)(2,1)S(1)}, bf16[2,1024,128]{2,1,0:T(8,128)(2,1)S(1)}, u32[]{:S(2)}, u32[]{:S(2)}) collective-permute-start(bf16[2,1024,128]{2,1,0:T(8,128)(2,1)S(1)} %pad_maximum_fusion), channel_id=1, source_target_pairs={{0,4},{4,0},{1,5},{5,1},{2,6},{6,2},{3,7},{7,3},{8,12},{12,8},{9,1... | collective-permute-start | bytes 1572872 | tf_op jit(solution)/shard_map/ppermute | solution.py:18
  32.6 1.3 collective-permute-start.3
  33.9 0.6 collective-permute-done.4
  34.5 6.4 %collective-permute-start.6 = (bf16[1024,128]{1,0:T(8,128)(2,1)S(1)}, bf16[1024,128]{1,0:T(8,128)(2,1)S(1)}, u32[]{:S(2)}, u32[]{:S(2)}) collective-permute-start(bf16[1024,128]{1,0:T(8,128)(2,1)S(1)} %collective-permute-done.4), channel_id=1, source_target_pairs={{0,4},{4,0},{1,5},{5,1},{2,6},{6,2},{3,7},{7,3},{8,12},{12,8},{9,1... | collective-permute-start | bytes 786440 | tf_op jit(solution)/shard_map/ppermute | solution.py:18
  41.0 0.8 fusion.3.slots
  41.8 0.7 collective-permute-done.3
  42.5 0.7 copy-done.1
  43.2 6.1 %shard_map.77 = bf16[4,1024,128]{2,1,0:T(8,128)(2,1)} custom-call(s32[8,16]{1,0:T(8,128)S(1)} %fusion.3.slots, bf16[8,128,128]{2,1,0:T(8,128)(2,1)} %bitcast.26, bf16[8,128,128]{2,1,0:T(8,128)(2,1)S(1)} %bitcast.22, bf16[8,128,128]{2,1,0:T(8,128)(2,1)S(1)} %bitcast.20, bf16[8,128,128]{2,1,0:T(8,128)(2,1)S(1)} %bitcast.18, bf16[8,128,128]{2,1,0:T(8,128)(2,1)S(1)} %bitcast.24, ...), custom_call_target="tpu_custom_call" | custom-call | flops 536870912 | bytes 7340032 | tf_op jit(solution)/shard_map/pallas_call | solution.py:97
  49.3 6.9 %all-to-all-start.1 = ((bf16[4,1024,128]{2,1,0:T(8,128)(2,1)}), bf16[4,1024,128]{2,1,0:T(8,128)(2,1)S(1)}, u32[]{:S(2)}, u32[]{:S(2)}) async-start(bf16[4,1024,128]{2,1,0:T(8,128)(2,1)} %shard_map.77), calls=%async_computation.1 | async-start | bytes 2097152 | tf_op jit(solution)/shard_map/all_to_all | solution.py:173
  56.3 19.0 %all-to-all-done.1.agg = bf16[4,1024,128]{2,1,0:T(8,128)(2,1)S(1)} async-done(((bf16[4,1024,128]{2,1,0:T(8,128)(2,1)}), bf16[4,1024,128]{2,1,0:T(8,128)(2,1)S(1)}, u32[]{:S(2)}, u32[]{:S(2)}) %all-to-all-start.1) | async-done | bytes 1048608 | tf_op jit(solution)/shard_map/all_to_all | solution.py:173
  75.2 3.2 %shard_map.78 = (bf16[1024,128]{1,0:T(8,128)(2,1)}, bf16[128,512]{1,0:T(8,128)(2,1)S(1)}) custom-call(s32[1]{0:T(128)} %bitcast.me, bf16[4,1024,128]{2,1,0:T(8,128)(2,1)S(1)} %all-to-all-done.1.agg, bf16[512,512]{1,0:T(8,128)(2,1)S(1)} %bitcast.16, bf16[1024,512]{1,0:T(8,128)(2,1)S(1)} %copy-done), custom_call_target="tpu_custom_call" | custom-call | tf_op jit(solution)/shard_map/pallas_call | solution.py:145
  78.5 25.9 %all_to_all.25 = bf16[16,8,512]{2,1,0:T(8,128)(2,1)S(1)} all-to-all(bf16[16,8,512]{2,1,0:T(8,128)(2,1)S(1)} %bitcast.25), channel_id=1, replica_groups=mesh['y_lo'=2,'x'=8,'z'=8,'core'=2,'col'=4] {'z','core'}, dimensions={0} | all-to-all | bytes 262144 | tf_op jit(solution)/shard_map/all_to_all | solution.py:173
  104.4 15.0 %all_to_all.26 = bf16[16,8,512]{2,1,0:T(8,128)(2,1)S(1)} all-to-all(bf16[16,8,512]{2,1,0:T(8,128)(2,1)S(1)} %broadcast_in_dim.21), channel_id=1, replica_groups=mesh['y_lo'=2,'x'=8,'z'=8,'core'=2,'col'=4] {'y_lo','x'}, dimensions={0} | all-to-all | bytes 262144 | tf_op jit(solution)/shard_map/all_to_all | solution.py:173
  119.5 13.1 %all_to_all.27 = bf16[16,8,512]{2,1,0:T(8,128)(2,1)S(1)} all-to-all(bf16[16,8,512]{2,1,0:T(8,128)(2,1)S(1)} %broadcast_in_dim.22), channel_id=1, replica_groups=mesh['y_lo'=2,'x'=8,'z'=8,'core'=2,'col'=4] {'z','core'}, dimensions={0} | all-to-all | bytes 262144 | tf_op jit(solution)/shard_map/all_to_all | solution.py:173
  132.5 0.7 bitcast_convert_fusion
  (11 shorter events, 0.1 us)
Async XLA Ops:
  0.6 17.4 %collective-permute-start = (bf16[1024,128]{1,0:T(8,128)(2,1)}, bf16[1024,128]{1,0:T(8,128)(2,1)S(1)}, u32[]{:S(2)}, u32[]{:S(2)}) collective-permute-start(bf16[1024,128]{1,0:T(8,128)(2,1)} %param.6), channel_id=1, source_target_pairs={{0,4},{4,0},{1,5},{5,1},{2,6},{6,2},{3,7},{7,3},{8,12},{12,8},{9,1... | collective-permute-start | bytes 786440 | tf_op jit(solution)/shard_map/ppermute | solution.py:18
  18.1 7.8 %collective-permute-start.2 = (bf16[1024,128]{1,0:T(8,128)(2,1)S(1)}, bf16[1024,128]{1,0:T(8,128)(2,1)S(1)}, u32[]{:S(2)}, u32[]{:S(2)}) collective-permute-start(bf16[1024,128]{1,0:T(8,128)(2,1)S(1)} %collective-permute-done), channel_id=1, source_target_pairs={{0,8},{8,16},{16,24},{24,32},{32,40},{40,48},{48,56},{56,64},{64,7... | collective-permute-start | bytes 786440 | tf_op jit(solution)/shard_map/ppermute | solution.py:25
  19.3 8.6 %collective-permute-start.1 = (bf16[1024,128]{1,0:T(8,128)(2,1)}, bf16[1024,128]{1,0:T(8,128)(2,1)S(1)}, u32[]{:S(2)}, u32[]{:S(2)}) collective-permute-start(bf16[1024,128]{1,0:T(8,128)(2,1)} %param.6), channel_id=1, source_target_pairs={{0,8},{8,16},{16,24},{24,32},{32,40},{40,48},{48,56},{56,64},{64,7... | collective-permute-start | bytes 786440 | tf_op jit(solution)/shard_map/ppermute | solution.py:25
  22.4 20.1 %all-to-all-start = ((bf16[4,128,512]{2,1,0:T(8,128)(2,1)}), bf16[4,128,512]{2,1,0:T(8,128)(2,1)S(1)}, u32[]{:S(2)}, u32[]{:S(2)}) async-start(bf16[4,128,512]{2,1,0:T(8,128)(2,1)} %broadcast_in_dim.20), calls=%async_computation | async-start | bytes 1048576 | tf_op jit(solution)/shard_map/all_to_all | solution.py:173
  25.9 8.7 %collective-permute-start.4 = (bf16[1024,128]{1,0:T(8,128)(2,1)S(1)}, bf16[1024,128]{1,0:T(8,128)(2,1)S(1)}, u32[]{:S(2)}, u32[]{:S(2)}) collective-permute-start(bf16[1024,128]{1,0:T(8,128)(2,1)S(1)} %collective-permute-done.2), channel_id=1, source_target_pairs={{0,8},{8,16},{16,24},{24,32},{32,40},{40,48},{48,56},{56,64},{64,7... | collective-permute-start | bytes 786440 | tf_op jit(solution)/shard_map/ppermute | solution.py:25
  28.0 14.5 %collective-permute-start.5 = (bf16[2,1024,128]{2,1,0:T(8,128)(2,1)S(1)}, bf16[2,1024,128]{2,1,0:T(8,128)(2,1)S(1)}, u32[]{:S(2)}, u32[]{:S(2)}) collective-permute-start(bf16[2,1024,128]{2,1,0:T(8,128)(2,1)S(1)} %pad_maximum_fusion), channel_id=1, source_target_pairs={{0,4},{4,0},{1,5},{5,1},{2,6},{6,2},{3,7},{7,3},{8,12},{12,8},{9,1... | collective-permute-start | bytes 1572872 | tf_op jit(solution)/shard_map/ppermute | solution.py:18
  32.6 9.9 %collective-permute-start.3 = (bf16[1024,128]{1,0:T(8,128)(2,1)S(1)}, bf16[1024,128]{1,0:T(8,128)(2,1)S(1)}, u32[]{:S(2)}, u32[]{:S(2)}) collective-permute-start(bf16[1024,128]{1,0:T(8,128)(2,1)S(1)} %collective-permute-done.1), channel_id=1, source_target_pairs={{0,8},{8,16},{16,24},{24,32},{32,40},{40,48},{48,56},{56,64},{64,7... | collective-permute-start | bytes 786440 | tf_op jit(solution)/shard_map/ppermute | solution.py:25
  34.5 8.0 %collective-permute-start.6 = (bf16[1024,128]{1,0:T(8,128)(2,1)S(1)}, bf16[1024,128]{1,0:T(8,128)(2,1)S(1)}, u32[]{:S(2)}, u32[]{:S(2)}) collective-permute-start(bf16[1024,128]{1,0:T(8,128)(2,1)S(1)} %collective-permute-done.4), channel_id=1, source_target_pairs={{0,4},{4,0},{1,5},{5,1},{2,6},{6,2},{3,7},{7,3},{8,12},{12,8},{9,1... | collective-permute-start | bytes 786440 | tf_op jit(solution)/shard_map/ppermute | solution.py:18
  42.5 0.7 copy-start.1
  43.2 32.0 %copy-start = (bf16[1024,512]{1,0:T(8,128)(2,1)S(1)}, bf16[1024,512]{1,0:T(8,128)(2,1)}, u32[]{:S(2)}) copy-start(bf16[1024,512]{1,0:T(8,128)(2,1)} %cotangent.1) | copy-start | bytes 3145732
  49.3 25.9 %all-to-all-start.1 = ((bf16[4,1024,128]{2,1,0:T(8,128)(2,1)}), bf16[4,1024,128]{2,1,0:T(8,128)(2,1)S(1)}, u32[]{:S(2)}, u32[]{:S(2)}) async-start(bf16[4,1024,128]{2,1,0:T(8,128)(2,1)} %shard_map.77), calls=%async_computation.1 | async-start | bytes 2097152 | tf_op jit(solution)/shard_map/all_to_all | solution.py:173

commit v6 on v4

--- a/solution.py
+++ b/solution.py
@@ -25,14 +25,11 @@
     return lax.ppermute(x, ROW, up + down)
 
 
-def halo(features, weight):
+def halo(features):
     other = swapped(features)
     one = passed_on(jnp.stack([features, other]))
     two = passed_on(one)
-    whole_weight = spread(weight, "col")
-    last = swapped(two[1] + whole_weight[0, 0, 0] * 0)
-    pieces = [(features, 0), (other, 1), (one, 2), (two, 4), (swapped(one), 6), (last, 8)]
-    return pieces, whole_weight.reshape(-1, weight.shape[1])
+    return [(features, 0), (other, 1), (one, 2), (two, 4), (swapped(one), 6), (swapped(two[1]), 8)]
 
 
 def slots_of(tile_cols, tile_count, blocks_here):
@@ -182,8 +179,8 @@
 def shards(features, tile_vals, tile_cols, tile_count, weight, cotangent):
     groups = lax.axis_size("col")
     slots = slots_of(tile_cols, tile_count, tile_vals.shape[0])
-    pieces, whole_weight = halo(features, weight)
-    aggregated = tiles(pieces, slots, tile_vals, groups)
+    whole_weight = spread(weight, "col").reshape(-1, weight.shape[1])
+    aggregated = tiles(halo(features), slots, tile_vals, groups)
     activated, part = dense(exchanged(aggregated, "col"), whole_weight, cotangent)
     return activated, summed_over_row(part)
 

time: 134 us -> 135 us (level)
  starting transfers between devices: 32.6 us -> 34.4 us
  waiting for transfers between devices: 28.2 us -> 29.9 us
    ppermute x2, waiting for transfers between devices: 3.54 us -> 8.63 us  [passed_on(): return lax.ppermute(x, ROW, up + down)]
    all_to_all x2, waiting for transfers between devices: 22.9 us -> 19.2 us  [exchanged(): return lax.all_to_all(x, axes, 0, 0, tiled=True)]
    all_to_all x2, starting transfers between devices: 7 us -> 10.4 us  [exchanged(): return lax.all_to_all(x, axes, 0, 0, tiled=True)]
    ppermute x3, starting transfers between devices: 23 us -> 21.4 us  [swapped(): return lax.ppermute(x, 'core', [(0, 1), (1, 0)])]
  transfers between devices with their start and end apart: 7 -> 7, of which waited for: 6 -> 4; matrix products, arithmetic and copies ran while one was open for 2% -> 2% of each run, Pallas kernels for 0% -> 4%
where the time goes in v6:
time: 135 us
  blocking collectives  56.9 us (42%)
  starting transfers between devices  34.4 us (25%)
  waiting for transfers between devices  29.9 us (22%)
  Pallas kernels  8.6 us (6%)
  other arithmetic  2.54 us (2%)
  local copies, waits for them, and re-layouts  1.8 us (1%)
    all_to_all x3, blocking collectives, exchanged(): return lax.all_to_all(x, axes, 0, 0, tiled=True)  56.9 us
    ppermute x3, starting transfers between devices, swapped(): return lax.ppermute(x, 'core', [(0, 1), (1, 0)])  21.4 us
    all_to_all x2, waiting for transfers between devices, exchanged(): return lax.all_to_all(x, axes, 0, 0, tiled=True)  19.2 us
    all_to_all x2, starting transfers between devices, exchanged(): return lax.all_to_all(x, axes, 0, 0, tiled=True)  10.4 us
    ppermute x2, waiting for transfers between devices, passed_on(): return lax.ppermute(x, ROW, up + down)  8.63 us
    pallas_call x1, Pallas kernels, tiles(): pl.pallas_call(functools.partial(tiles_kernel, starts), out_shape=jax.Sha...  5.35 us
    pallas_call x1, Pallas kernels, dense(): pl.pallas_call(dense_kernel, out_shape=(jax.ShapeDtypeStruct((rows, f_out...  3.24 us
  transfers between devices with their start and end apart: 7, of which 4 were waited for; matrix products, arithmetic and copies ran while one was open for 2% of the time, Pallas kernels for 4%

profile of v6, /device:TPU:1, one launch (start us, length us, event | category | flops | bytes accessed | tf_op | source)
XLA Modules:
  0.0 134.9 jit_solution(11806995897720604727)
XLA Ops:
  0.6 16.1 %collective-permute-start = (bf16[1024,128]{1,0:T(8,128)(2,1)}, bf16[1024,128]{1,0:T(8,128)(2,1)S(1)}, u32[]{:S(2)}, u32[]{:S(2)}) collective-permute-start(bf16[1024,128]{1,0:T(8,128)(2,1)} %param.6), channel_id=1, source_target_pairs={{0,4},{4,0},{1,5},{5,1},{2,6},{6,2},{3,7},{7,3},{8,12},{12,8},{9,1... | collective-permute-start | bytes 786440 | tf_op jit(solution)/shard_map/ppermute | solution.py:18
  16.7 1.4 %collective-permute-done = bf16[1024,128]{1,0:T(8,128)(2,1)S(1)} collective-permute-done((bf16[1024,128]{1,0:T(8,128)(2,1)}, bf16[1024,128]{1,0:T(8,128)(2,1)S(1)}, u32[]{:S(2)}, u32[]{:S(2)}) %collective-permute-start) | collective-permute-done | bytes 262176 | tf_op jit(solution)/shard_map/ppermute | solution.py:18
  18.1 1.0 pad_maximum_fusion
  19.1 1.3 collective-permute-start.1
  20.4 8.6 %collective-permute-done.1 = bf16[2,1024,128]{2,1,0:T(8,128)(2,1)S(1)} collective-permute-done((bf16[2,1024,128]{2,1,0:T(8,128)(2,1)S(1)}, bf16[2,1024,128]{2,1,0:T(8,128)(2,1)S(1)}, u32[]{:S(2)}, u32[]{:S(2)}) %collective-permute-start.1) | collective-permute-done | bytes 524320 | tf_op jit(solution)/shard_map/ppermute | solution.py:25
  29.0 1.3 collective-permute-start.2
  30.3 1.7 %broadcast_in_dim.20 = bf16[4,128,512]{2,1,0:T(8,128)(2,1)} broadcast(bf16[128,512]{1,0:T(8,128)(2,1)} %param.10), dimensions={1,2} | broadcast | bytes 655360 | tf_op jit(solution)/shard_map/broadcast_in_dim | solution.py:163
  32.0 3.5 %all-to-all-start.1 = ((bf16[4,128,512]{2,1,0:T(8,128)(2,1)}), bf16[4,128,512]{2,1,0:T(8,128)(2,1)S(1)}, u32[]{:S(2)}, u32[]{:S(2)}) async-start(bf16[4,128,512]{2,1,0:T(8,128)(2,1)} %broadcast_in_dim.20), calls=%async_computation.1 | async-start | bytes 1048576 | tf_op jit(solution)/shard_map/all_to_all | solution.py:167
  35.5 3.5 %collective-permute-start.3 = (bf16[2,1024,128]{2,1,0:T(8,128)(2,1)S(1)}, bf16[2,1024,128]{2,1,0:T(8,128)(2,1)S(1)}, u32[]{:S(2)}, u32[]{:S(2)}) collective-permute-start(bf16[2,1024,128]{2,1,0:T(8,128)(2,1)S(1)} %collective-permute-done.1), channel_id=1, source_target_pairs={{0,4},{4,0},{1,5},{5,1},{2,6},{6,2},{3,7},{7,3},{8,12},{12,8},{9,1... | collective-permute-start | bytes 1572872 | tf_op jit(solution)/shard_map/ppermute | solution.py:18
  39.0 0.0 collective-permute-done.2
  39.0 1.9 %collective-permute-start.4 = (bf16[1024,128]{1,0:T(8,128)(2,1)S(1)}, bf16[1024,128]{1,0:T(8,128)(2,1)S(1)}, u32[]{:S(2)}, u32[]{:S(2)}) collective-permute-start(bf16[1024,128]{1,0:T(8,128)(2,1)S(1)} %slice_bitcast_fusion), channel_id=1, source_target_pairs={{0,4},{4,0},{1,5},{5,1},{2,6},{6,2},{3,7},{7,3},{8,12},{12,8},{9,1... | collective-permute-start | bytes 786440 | tf_op jit(solution)/shard_map/ppermute | solution.py:18
  41.0 0.8 fusion.3.slots
  41.7 0.0 collective-permute-done.3
  41.7 0.7 collective-permute-done.4
  42.4 5.4 %shard_map.77 = bf16[4,1024,128]{2,1,0:T(8,128)(2,1)} custom-call(s32[8,16]{1,0:T(8,128)S(1)} %fusion.3.slots, bf16[8,128,128]{2,1,0:T(8,128)(2,1)} %bitcast.24, bf16[8,128,128]{2,1,0:T(8,128)(2,1)S(1)} %bitcast.19, bf16[16,128,128]{2,1,0:T(8,128)(2,1)} %bitcast.25, bf16[16,128,128]{2,1,0:T(8,128)(2,1)S(1)} %bitcast.17, bf16[16,128,128]{2,1,0:T(8,128)(2,1)S(1)} %bitcast.20, ...), custom_call_target="tpu_custom_call" | custom-call | flops 536870912 | bytes 7340032 | tf_op jit(solution)/shard_map/pallas_call | solution.py:91
  47.8 0.0 all-to-all-done.1
  47.8 6.9 %all-to-all-start = ((bf16[4,1024,128]{2,1,0:T(8,128)(2,1)}), bf16[4,1024,128]{2,1,0:T(8,128)(2,1)S(1)}, u32[]{:S(2)}, u32[]{:S(2)}) async-start(bf16[4,1024,128]{2,1,0:T(8,128)(2,1)} %shard_map.77), calls=%async_computation | async-start | bytes 2097152 | tf_op jit(solution)/shard_map/all_to_all | solution.py:167
  54.7 19.2 %all-to-all-done.agg = bf16[4,1024,128]{2,1,0:T(8,128)(2,1)S(1)} async-done(((bf16[4,1024,128]{2,1,0:T(8,128)(2,1)}), bf16[4,1024,128]{2,1,0:T(8,128)(2,1)S(1)}, u32[]{:S(2)}, u32[]{:S(2)}) %all-to-all-start) | async-done | bytes 1048608 | tf_op jit(solution)/shard_map/all_to_all | solution.py:167
  73.9 0.0 copy-done
  73.9 3.2 %shard_map.78 = (bf16[1024,128]{1,0:T(8,128)(2,1)}, bf16[128,512]{1,0:T(8,128)(2,1)S(1)}) custom-call(s32[1]{0:T(128)} %bitcast.me, bf16[4,1024,128]{2,1,0:T(8,128)(2,1)S(1)} %all-to-all-done.agg, bf16[512,512]{1,0:T(8,128)(2,1)S(1)} %bitcast.16, bf16[1024,512]{1,0:T(8,128)(2,1)S(1)} %copy-done), custom_call_target="tpu_custom_call" | custom-call | tf_op jit(solution)/shard_map/pallas_call | solution.py:139
  77.1 29.8 %all_to_all.25 = bf16[16,8,512]{2,1,0:T(8,128)(2,1)S(1)} all-to-all(bf16[16,8,512]{2,1,0:T(8,128)(2,1)S(1)} %bitcast.22), channel_id=1, replica_groups=mesh['y_lo'=2,'x'=8,'z'=8,'core'=2,'col'=4] {'z','core'}, dimensions={0} | all-to-all | bytes 262144 | tf_op jit(solution)/shard_map/all_to_all | solution.py:167
  107.0 14.1 %all_to_all.26 = bf16[16,8,512]{2,1,0:T(8,128)(2,1)S(1)} all-to-all(bf16[16,8,512]{2,1,0:T(8,128)(2,1)S(1)} %broadcast_in_dim.21), channel_id=1, replica_groups=mesh['y_lo'=2,'x'=8,'z'=8,'core'=2,'col'=4] {'y_lo','x'}, dimensions={0} | all-to-all | bytes 262144 | tf_op jit(solution)/shard_map/all_to_all | solution.py:167
  121.1 13.0 %all_to_all.27 = bf16[16,8,512]{2,1,0:T(8,128)(2,1)S(1)} all-to-all(bf16[16,8,512]{2,1,0:T(8,128)(2,1)S(1)} %broadcast_in_dim.22), channel_id=1, replica_groups=mesh['y_lo'=2,'x'=8,'z'=8,'core'=2,'col'=4] {'z','core'}, dimensions={0} | all-to-all | bytes 262144 | tf_op jit(solution)/shard_map/all_to_all | solution.py:167
  134.1 0.7 bitcast_convert_fusion
  (8 shorter events, 0.1 us)
Async XLA Ops:
  0.6 17.4 %collective-permute-start = (bf16[1024,128]{1,0:T(8,128)(2,1)}, bf16[1024,128]{1,0:T(8,128)(2,1)S(1)}, u32[]{:S(2)}, u32[]{:S(2)}) collective-permute-start(bf16[1024,128]{1,0:T(8,128)(2,1)} %param.6), channel_id=1, source_target_pairs={{0,4},{4,0},{1,5},{5,1},{2,6},{6,2},{3,7},{7,3},{8,12},{12,8},{9,1... | collective-permute-start | bytes 786440 | tf_op jit(solution)/shard_map/ppermute | solution.py:18
  19.1 9.9 %collective-permute-start.1 = (bf16[2,1024,128]{2,1,0:T(8,128)(2,1)S(1)}, bf16[2,1024,128]{2,1,0:T(8,128)(2,1)S(1)}, u32[]{:S(2)}, u32[]{:S(2)}) collective-permute-start(bf16[2,1024,128]{2,1,0:T(8,128)(2,1)S(1)} %pad_maximum_fusion), channel_id=1, source_target_pairs={{0,8},{8,16},{16,24},{24,32},{32,40},{40,48},{48,56},{56,64},{64,7... | collective-permute-start | bytes 1572872 | tf_op jit(solution)/shard_map/ppermute | solution.py:25
  29.0 13.5 %copy-start.1 = (bf16[2,1024,128]{2,1,0:T(8,128)(2,1)}, bf16[2,1024,128]{2,1,0:T(8,128)(2,1)S(1)}, u32[]{:S(2)}) copy-start(bf16[2,1024,128]{2,1,0:T(8,128)(2,1)S(1)} %collective-permute-done.1) | copy-start | bytes 1572868
  29.0 10.0 %collective-permute-start.2 = (bf16[2,1024,128]{2,1,0:T(8,128)(2,1)S(1)}, bf16[2,1024,128]{2,1,0:T(8,128)(2,1)S(1)}, u32[]{:S(2)}, u32[]{:S(2)}) collective-permute-start(bf16[2,1024,128]{2,1,0:T(8,128)(2,1)S(1)} %collective-permute-done.1), channel_id=1, source_target_pairs={{0,8},{8,16},{16,24},{24,32},{32,40},{40,48},{48,56},{56,64},{64,7... | collective-permute-start | bytes 1572872 | tf_op jit(solution)/shard_map/ppermute | solution.py:25
  32.0 15.8 %all-to-all-start.1 = ((bf16[4,128,512]{2,1,0:T(8,128)(2,1)}), bf16[4,128,512]{2,1,0:T(8,128)(2,1)S(1)}, u32[]{:S(2)}, u32[]{:S(2)}) async-start(bf16[4,128,512]{2,1,0:T(8,128)(2,1)} %broadcast_in_dim.20), calls=%async_computation.1 | async-start | bytes 1048576 | tf_op jit(solution)/shard_map/all_to_all | solution.py:167
  35.5 6.2 %collective-permute-start.3 = (bf16[2,1024,128]{2,1,0:T(8,128)(2,1)S(1)}, bf16[2,1024,128]{2,1,0:T(8,128)(2,1)S(1)}, u32[]{:S(2)}, u32[]{:S(2)}) collective-permute-start(bf16[2,1024,128]{2,1,0:T(8,128)(2,1)S(1)} %collective-permute-done.1), channel_id=1, source_target_pairs={{0,4},{4,0},{1,5},{5,1},{2,6},{6,2},{3,7},{7,3},{8,12},{12,8},{9,1... | collective-permute-start | bytes 1572872 | tf_op jit(solution)/shard_map/ppermute | solution.py:18
  39.0 3.4 %collective-permute-start.4 = (bf16[1024,128]{1,0:T(8,128)(2,1)S(1)}, bf16[1024,128]{1,0:T(8,128)(2,1)S(1)}, u32[]{:S(2)}, u32[]{:S(2)}) collective-permute-start(bf16[1024,128]{1,0:T(8,128)(2,1)S(1)} %slice_bitcast_fusion), channel_id=1, source_target_pairs={{0,4},{4,0},{1,5},{5,1},{2,6},{6,2},{3,7},{7,3},{8,12},{12,8},{9,1... | collective-permute-start | bytes 786440 | tf_op jit(solution)/shard_map/ppermute | solution.py:18
  42.4 31.5 %copy-start = (bf16[1024,512]{1,0:T(8,128)(2,1)S(1)}, bf16[1024,512]{1,0:T(8,128)(2,1)}, u32[]{:S(2)}) copy-start(bf16[1024,512]{1,0:T(8,128)(2,1)} %cotangent.1) | copy-start | bytes 3145732
  47.8 26.1 %all-to-all-start = ((bf16[4,1024,128]{2,1,0:T(8,128)(2,1)}), bf16[4,1024,128]{2,1,0:T(8,128)(2,1)S(1)}, u32[]{:S(2)}, u32[]{:S(2)}) async-start(bf16[4,1024,128]{2,1,0:T(8,128)(2,1)} %shard_map.77), calls=%async_computation | async-start | bytes 2097152 | tf_op jit(solution)/shard_map/all_to_all | solution.py:167

commit v7 on v4

--- a/solution.py
+++ b/solution.py
@@ -62,8 +62,11 @@
     ]
     for copy in copies:
         copy.start()
+    span = blocks // vals_sems.shape[0]
+    parts = [pl.ds(i * span, span) for i in range(vals_sems.shape[0])]
     fetches = [
-        pltpu.make_async_copy(vals_hbm.at[b], vals.at[b], vals_sems.at[b]) for b in range(blocks)
+        pltpu.make_async_copy(vals_hbm.at[part], vals.at[part], vals_sems.at[i])
+        for i, part in enumerate(parts)
     ]
     for fetch in fetches:
         fetch.start()
@@ -71,7 +74,8 @@
     for copy in copies:
         copy.wait()
     for b in range(blocks):
-        fetches[b].wait()
+        if b % span == 0:
+            fetches[b // span].wait()
         total = jnp.zeros((tile, cols), F32)
         for t in range(0, count, 2):
             pair = jnp.concatenate([vals[b, t], vals[b, t + 1]], axis=1)
@@ -100,7 +104,7 @@
             pltpu.VMEM((9 * blocks + 1, tile, cols), BF16),
             pltpu.VMEM(tile_vals.shape, BF16),
             pltpu.SemaphoreType.DMA((len(arrays),)),
-            pltpu.SemaphoreType.DMA((blocks,)),
+            pltpu.SemaphoreType.DMA((blocks // 2,)),
         ],
         compiler_params=pltpu.CompilerParams(vmem_limit_bytes=16 << 20),
         cost_estimate=pl.CostEstimate(
@@ -137,7 +141,7 @@
 def dense(agg, weight, cotangent):
     groups, rows, width = agg.shape
     f_out = weight.shape[1]
-    block = 256
+    block = 512
     me = lax.axis_index("col").astype(jnp.int32)[None]
     return pl.pallas_call(
         dense_kernel,

time: 134 us -> 133 us (level)
  no operation moved by 1% of the time
where the time goes in v7:
time: 133 us; the launch traced here: 132 us
  blocking collectives  57.8 us (43%)
  starting transfers between devices  32.6 us (25%)
  waiting for transfers between devices  28.2 us (21%)
  Pallas kernels  7.43 us (6%)
  other arithmetic  2.56 us (2%)
  local copies, waits for them, and re-layouts  2.28 us (2%)
  between operations  1.41 us (1%)
    all_to_all x3, blocking collectives, exchanged(): return lax.all_to_all(x, axes, 0, 0, tiled=True)  57.8 us
    ppermute x3, starting transfers between devices, swapped(): return lax.ppermute(x, 'core', [(0, 1), (1, 0)])  23 us
    all_to_all x2, waiting for transfers between devices, exchanged(): return lax.all_to_all(x, axes, 0, 0, tiled=True)  22.9 us
    all_to_all x2, starting transfers between devices, exchanged(): return lax.all_to_all(x, axes, 0, 0, tiled=True)  7 us
    pallas_call x1, Pallas kernels, tiles(): pl.pallas_call(functools.partial(tiles_kernel, starts), out_shape=jax.Sha...  4.87 us
    ppermute x2, waiting for transfers between devices, passed_on(): return lax.ppermute(x, ROW, up + down)  3.54 us
  transfers between devices with their start and end apart: 7, of which 6 were waited for; matrix products, arithmetic and copies ran while one was open for 2% of the time, Pallas kernels for 0%

profile of v7, /device:TPU:1, one launch (start us, length us, event | category | flops | bytes accessed | tf_op | source)
XLA Modules:
  0.0 132.2 jit_solution(15763840477047366913)
XLA Ops:
  0.6 16.1 %collective-permute-start = (bf16[1024,128]{1,0:T(8,128)(2,1)}, bf16[1024,128]{1,0:T(8,128)(2,1)S(1)}, u32[]{:S(2)}, u32[]{:S(2)}) collective-permute-start(bf16[1024,128]{1,0:T(8,128)(2,1)} %param.6), channel_id=1, source_target_pairs={{0,4},{4,0},{1,5},{5,1},{2,6},{6,2},{3,7},{7,3},{8,12},{12,8},{9,1... | collective-permute-start | bytes 786440 | tf_op jit(solution)/shard_map/ppermute | solution.py:18
  16.7 1.4 %collective-permute-done = bf16[1024,128]{1,0:T(8,128)(2,1)S(1)} collective-permute-done((bf16[1024,128]{1,0:T(8,128)(2,1)}, bf16[1024,128]{1,0:T(8,128)(2,1)S(1)}, u32[]{:S(2)}, u32[]{:S(2)}) %collective-permute-start) | collective-permute-done | bytes 262176 | tf_op jit(solution)/shard_map/ppermute | solution.py:18
  18.1 1.0 pad_maximum_fusion
  19.1 1.3 collective-permute-start.1
  20.4 1.7 %broadcast_in_dim.20 = bf16[4,128,512]{2,1,0:T(8,128)(2,1)} broadcast(bf16[128,512]{1,0:T(8,128)(2,1)} %param.10), dimensions={1,2} | broadcast | bytes 655360 | tf_op jit(solution)/shard_map/broadcast_in_dim | solution.py:170
  22.1 3.5 %all-to-all-start = ((bf16[4,128,512]{2,1,0:T(8,128)(2,1)}), bf16[4,128,512]{2,1,0:T(8,128)(2,1)S(1)}, u32[]{:S(2)}, u32[]{:S(2)}) async-start(bf16[4,128,512]{2,1,0:T(8,128)(2,1)} %broadcast_in_dim.20), calls=%async_computation | async-start | bytes 1048576 | tf_op jit(solution)/shard_map/all_to_all | solution.py:174
  25.6 3.4 %collective-permute-done.1 = bf16[2,1024,128]{2,1,0:T(8,128)(2,1)S(1)} collective-permute-done((bf16[2,1024,128]{2,1,0:T(8,128)(2,1)S(1)}, bf16[2,1024,128]{2,1,0:T(8,128)(2,1)S(1)}, u32[]{:S(2)}, u32[]{:S(2)}) %collective-permute-start.1) | collective-permute-done | bytes 524320 | tf_op jit(solution)/shard_map/ppermute | solution.py:25
  29.0 1.3 collective-permute-start.2
  30.3 3.5 %collective-permute-start.3 = (bf16[2,1024,128]{2,1,0:T(8,128)(2,1)S(1)}, bf16[2,1024,128]{2,1,0:T(8,128)(2,1)S(1)}, u32[]{:S(2)}, u32[]{:S(2)}) collective-permute-start(bf16[2,1024,128]{2,1,0:T(8,128)(2,1)S(1)} %collective-permute-done.1), channel_id=1, source_target_pairs={{0,4},{4,0},{1,5},{5,1},{2,6},{6,2},{3,7},{7,3},{8,12},{12,8},{9,1... | collective-permute-start | bytes 1572872 | tf_op jit(solution)/shard_map/ppermute | solution.py:18
  33.7 3.9 %all-to-all-done = bf16[4,128,512]{2,1,0:T(8,128)(2,1)S(1)} async-done(((bf16[4,128,512]{2,1,0:T(8,128)(2,1)}), bf16[4,128,512]{2,1,0:T(8,128)(2,1)S(1)}, u32[]{:S(2)}, u32[]{:S(2)}) %all-to-all-start) | async-done | bytes 524320 | tf_op jit(solution)/shard_map/all_to_all | solution.py:174
  37.6 0.5 slice.9
  38.8 0.1 collective-permute-done.2
  38.9 3.5 %collective-permute-start.4 = (bf16[1024,128]{1,0:T(8,128)(2,1)S(1)}, bf16[1024,128]{1,0:T(8,128)(2,1)S(1)}, u32[]{:S(2)}, u32[]{:S(2)}) collective-permute-start(bf16[1024,128]{1,0:T(8,128)(2,1)S(1)} %fusion), channel_id=1, source_target_pairs={{0,4},{4,0},{1,5},{5,1},{2,6},{6,2},{3,7},{7,3},{8,12},{12,8},{9,1... | collective-permute-start | bytes 786440 | tf_op jit(solution)/shard_map/ppermute | solution.py:18
  42.4 0.8 fusion.4.slots
  43.2 0.0 collective-permute-done.3
  43.2 0.3 collective-permute-done.4
  43.5 4.9 %shard_map.77 = bf16[4,1024,128]{2,1,0:T(8,128)(2,1)} custom-call(s32[8,16]{1,0:T(8,128)S(1)} %fusion.4.slots, bf16[8,128,128]{2,1,0:T(8,128)(2,1)} %bitcast.25, bf16[8,128,128]{2,1,0:T(8,128)(2,1)S(1)} %bitcast.20, bf16[16,128,128]{2,1,0:T(8,128)(2,1)} %bitcast.26, bf16[16,128,128]{2,1,0:T(8,128)(2,1)S(1)} %bitcast.18, bf16[16,128,128]{2,1,0:T(8,128)(2,1)S(1)} %bitcast.21, ...), custom_call_target="tpu_custom_call" | custom-call | flops 536870912 | bytes 7340032 | tf_op jit(solution)/shard_map/pallas_call | solution.py:98
  48.4 3.5 %all-to-all-start.1 = ((bf16[4,1024,128]{2,1,0:T(8,128)(2,1)}), bf16[4,1024,128]{2,1,0:T(8,128)(2,1)S(1)}, u32[]{:S(2)}, u32[]{:S(2)}) async-start(bf16[4,1024,128]{2,1,0:T(8,128)(2,1)} %shard_map.77), calls=%async_computation.1 | async-start | bytes 2097152 | tf_op jit(solution)/shard_map/all_to_all | solution.py:174
  52.0 19.1 %all-to-all-done.1.agg = bf16[4,1024,128]{2,1,0:T(8,128)(2,1)S(1)} async-done(((bf16[4,1024,128]{2,1,0:T(8,128)(2,1)}), bf16[4,1024,128]{2,1,0:T(8,128)(2,1)S(1)}, u32[]{:S(2)}, u32[]{:S(2)}) %all-to-all-start.1) | async-done | bytes 1048608 | tf_op jit(solution)/shard_map/all_to_all | solution.py:174
  71.0 2.6 %shard_map.78 = (bf16[1024,128]{1,0:T(8,128)(2,1)}, bf16[128,512]{1,0:T(8,128)(2,1)S(1)}) custom-call(s32[1]{0:T(128)} %bitcast.me, bf16[4,1024,128]{2,1,0:T(8,128)(2,1)S(1)} %all-to-all-done.1.agg, bf16[512,512]{1,0:T(8,128)(2,1)S(1)} %bitcast.17, bf16[1024,512]{1,0:T(8,128)(2,1)S(1)} %copy-done), custom_call_target="tpu_custom_call" | custom-call | tf_op jit(solution)/shard_map/pallas_call | solution.py:146
  73.6 31.2 %all_to_all.25 = bf16[16,8,512]{2,1,0:T(8,128)(2,1)S(1)} all-to-all(bf16[16,8,512]{2,1,0:T(8,128)(2,1)S(1)} %bitcast.23), channel_id=1, replica_groups=mesh['y_lo'=2,'x'=8,'z'=8,'core'=2,'col'=4] {'z','core'}, dimensions={0} | all-to-all | bytes 262144 | tf_op jit(solution)/shard_map/all_to_all | solution.py:174
  104.8 13.5 %all_to_all.26 = bf16[16,8,512]{2,1,0:T(8,128)(2,1)S(1)} all-to-all(bf16[16,8,512]{2,1,0:T(8,128)(2,1)S(1)} %broadcast_in_dim.21), channel_id=1, replica_groups=mesh['y_lo'=2,'x'=8,'z'=8,'core'=2,'col'=4] {'y_lo','x'}, dimensions={0} | all-to-all | bytes 262144 | tf_op jit(solution)/shard_map/all_to_all | solution.py:174
  118.4 13.1 %all_to_all.27 = bf16[16,8,512]{2,1,0:T(8,128)(2,1)S(1)} all-to-all(bf16[16,8,512]{2,1,0:T(8,128)(2,1)S(1)} %broadcast_in_dim.22), channel_id=1, replica_groups=mesh['y_lo'=2,'x'=8,'z'=8,'core'=2,'col'=4] {'z','core'}, dimensions={0} | all-to-all | bytes 262144 | tf_op jit(solution)/shard_map/all_to_all | solution.py:174
  131.5 0.7 bitcast_convert_fusion
  (9 shorter events, 0.1 us)
Async XLA Ops:
  0.6 17.4 %collective-permute-start = (bf16[1024,128]{1,0:T(8,128)(2,1)}, bf16[1024,128]{1,0:T(8,128)(2,1)S(1)}, u32[]{:S(2)}, u32[]{:S(2)}) collective-permute-start(bf16[1024,128]{1,0:T(8,128)(2,1)} %param.6), channel_id=1, source_target_pairs={{0,4},{4,0},{1,5},{5,1},{2,6},{6,2},{3,7},{7,3},{8,12},{12,8},{9,1... | collective-permute-start | bytes 786440 | tf_op jit(solution)/shard_map/ppermute | solution.py:18
  19.1 9.9 %collective-permute-start.1 = (bf16[2,1024,128]{2,1,0:T(8,128)(2,1)S(1)}, bf16[2,1024,128]{2,1,0:T(8,128)(2,1)S(1)}, u32[]{:S(2)}, u32[]{:S(2)}) collective-permute-start(bf16[2,1024,128]{2,1,0:T(8,128)(2,1)S(1)} %pad_maximum_fusion), channel_id=1, source_target_pairs={{0,8},{8,16},{16,24},{24,32},{32,40},{40,48},{48,56},{56,64},{64,7... | collective-permute-start | bytes 1572872 | tf_op jit(solution)/shard_map/ppermute | solution.py:25
  22.1 15.5 %all-to-all-start = ((bf16[4,128,512]{2,1,0:T(8,128)(2,1)}), bf16[4,128,512]{2,1,0:T(8,128)(2,1)S(1)}, u32[]{:S(2)}, u32[]{:S(2)}) async-start(bf16[4,128,512]{2,1,0:T(8,128)(2,1)} %broadcast_in_dim.20), calls=%async_computation | async-start | bytes 1048576 | tf_op jit(solution)/shard_map/all_to_all | solution.py:174
  29.0 14.5 %copy-start.1 = (bf16[2,1024,128]{2,1,0:T(8,128)(2,1)}, bf16[2,1024,128]{2,1,0:T(8,128)(2,1)S(1)}, u32[]{:S(2)}) copy-start(bf16[2,1024,128]{2,1,0:T(8,128)(2,1)S(1)} %collective-permute-done.1) | copy-start | bytes 1572868
  29.0 9.9 %collective-permute-start.2 = (bf16[2,1024,128]{2,1,0:T(8,128)(2,1)S(1)}, bf16[2,1024,128]{2,1,0:T(8,128)(2,1)S(1)}, u32[]{:S(2)}, u32[]{:S(2)}) collective-permute-start(bf16[2,1024,128]{2,1,0:T(8,128)(2,1)S(1)} %collective-permute-done.1), channel_id=1, source_target_pairs={{0,8},{8,16},{16,24},{24,32},{32,40},{40,48},{48,56},{56,64},{64,7... | collective-permute-start | bytes 1572872 | tf_op jit(solution)/shard_map/ppermute | solution.py:25
  30.3 12.9 %collective-permute-start.3 = (bf16[2,1024,128]{2,1,0:T(8,128)(2,1)S(1)}, bf16[2,1024,128]{2,1,0:T(8,128)(2,1)S(1)}, u32[]{:S(2)}, u32[]{:S(2)}) collective-permute-start(bf16[2,1024,128]{2,1,0:T(8,128)(2,1)S(1)} %collective-permute-done.1), channel_id=1, source_target_pairs={{0,4},{4,0},{1,5},{5,1},{2,6},{6,2},{3,7},{7,3},{8,12},{12,8},{9,1... | collective-permute-start | bytes 1572872 | tf_op jit(solution)/shard_map/ppermute | solution.py:18
  38.9 4.6 %collective-permute-start.4 = (bf16[1024,128]{1,0:T(8,128)(2,1)S(1)}, bf16[1024,128]{1,0:T(8,128)(2,1)S(1)}, u32[]{:S(2)}, u32[]{:S(2)}) collective-permute-start(bf16[1024,128]{1,0:T(8,128)(2,1)S(1)} %fusion), channel_id=1, source_target_pairs={{0,4},{4,0},{1,5},{5,1},{2,6},{6,2},{3,7},{7,3},{8,12},{12,8},{9,1... | collective-permute-start | bytes 786440 | tf_op jit(solution)/shard_map/ppermute | solution.py:18
  43.5 27.5 %copy-start = (bf16[1024,512]{1,0:T(8,128)(2,1)S(1)}, bf16[1024,512]{1,0:T(8,128)(2,1)}, u32[]{:S(2)}) copy-start(bf16[1024,512]{1,0:T(8,128)(2,1)} %cotangent.1) | copy-start | bytes 3145732
  48.4 22.6 %all-to-all-start.1 = ((bf16[4,1024,128]{2,1,0:T(8,128)(2,1)}), bf16[4,1024,128]{2,1,0:T(8,128)(2,1)S(1)}, u32[]{:S(2)}, u32[]{:S(2)}) async-start(bf16[4,1024,128]{2,1,0:T(8,128)(2,1)} %shard_map.77), calls=%async_computation.1 | async-start | bytes 2097152 | tf_op jit(solution)/shard_map/all_to_all | solution.py:174

commit v8 on v7

--- a/solution.py
+++ b/solution.py
@@ -81,12 +81,10 @@
             pair = jnp.concatenate([vals[b, t], vals[b, t + 1]], axis=1)
             rows = jnp.concatenate([window[slots[b, t]], window[slots[b, t + 1]]], axis=0)
             total += jnp.dot(pair, rows, preferred_element_type=F32)
-        done = total.astype(out.dtype)
-        for k in range(out.shape[0]):
-            out[k, pl.ds(b * tile, tile), :] = done
-
-
-def tiles(pieces, slots, tile_vals, times):
+        out[pl.ds(b * tile, tile), :] = total.astype(out.dtype)
+
+
+def tiles(pieces, slots, tile_vals):
     blocks, count, tile, _ = tile_vals.shape
     cols = pieces[0][0].shape[-1]
     arrays = [x.reshape(-1, tile, cols) for x, _ in pieces]
@@ -97,7 +95,7 @@
     hbm = pl.BlockSpec(memory_space=pltpu.HBM)
     return pl.pallas_call(
         functools.partial(tiles_kernel, starts),
-        out_shape=jax.ShapeDtypeStruct((times, blocks * tile, cols), BF16),
+        out_shape=jax.ShapeDtypeStruct((blocks * tile, cols), BF16),
         in_specs=[pl.BlockSpec(memory_space=pltpu.SMEM)] + [anywhere] * len(arrays) + [hbm],
         out_specs=pl.BlockSpec(memory_space=pltpu.VMEM),
         scratch_shapes=[
@@ -113,17 +111,27 @@
     )(slots, *arrays, pltpu.with_memory_space_constraint(tile_vals, pltpu.HBM))
 
 
-def dense_kernel(me, agg, weight, cotangent, activated, grad, act, total):
+def dense_kernel(me, weight, cotangent, *refs):
+    groups = weight.shape[0] // refs[0].shape[1]
+    aggs = refs[:groups]
+    activated, grad, turned, act, total = refs[groups:]
     step = pl.program_id(0)
     mine = me[0]
     width = activated.shape[1]
-    joined = jnp.concatenate([agg[k] for k in range(agg.shape[0])], axis=1)
-    pre = jnp.dot(joined, weight[...], preferred_element_type=F32)
+
+    @pl.when(step == 0)
+    def _():
+        for by in range(groups):
+            start = pl.multiple_of(lax.rem(mine + by, groups) * width, width)
+            turned[pl.ds(by * width, width), :] = weight[pl.ds(start, width), :]
+
+    joined = jnp.concatenate([agg[...] for agg in aggs], axis=1)
+    pre = jnp.dot(joined, turned[...], preferred_element_type=F32)
     sigma = 0.5 * jnp.tanh(0.5 * pre) + 0.5
     act[...] = pre * sigma
     activated[...] = act[:, pl.ds(pl.multiple_of(mine * width, width), width)].astype(BF16)
     dpre = (cotangent[...].astype(F32) * sigma * (1.0 + pre * (1.0 - sigma))).astype(BF16)
-    part = lax.dot_general(agg[mine], dpre, (((0,), (0,)), ((), ())), preferred_element_type=F32)
+    part = lax.dot_general(aggs[0][...], dpre, (((0,), (0,)), ((), ())), preferred_element_type=F32)
 
     @pl.when(step == 0)
     def _():
@@ -138,8 +146,8 @@
         grad[...] = total[...].astype(BF16)
 
 
-def dense(agg, weight, cotangent):
-    groups, rows, width = agg.shape
+def dense(aggs, weight, cotangent):
+    groups, (rows, width) = len(aggs), aggs[0].shape
     f_out = weight.shape[1]
     block = 512
     me = lax.axis_index("col").astype(jnp.int32)[None]
@@ -152,17 +160,26 @@
         grid=(rows // block,),
         in_specs=[
             pl.BlockSpec(memory_space=pltpu.SMEM),
-            pl.BlockSpec((groups, block, width), lambda i: (0, i, 0)),
             pl.BlockSpec((groups * width, f_out), lambda i: (0, 0)),
             pl.BlockSpec((block, f_out), lambda i: (i, 0)),
-        ],
+        ]
+        + [pl.BlockSpec((block, width), lambda i: (i, 0))] * groups,
         out_specs=(
             pl.BlockSpec((block, f_out // groups), lambda i: (i, 0)),
             pl.BlockSpec((width, f_out), lambda i: (0, 0)),
         ),
-        scratch_shapes=[pltpu.VMEM((block, f_out), F32), pltpu.VMEM((width, f_out), F32)],
+        scratch_shapes=[
+            pltpu.VMEM((groups * width, f_out), BF16),
+            pltpu.VMEM((block, f_out), F32),
+            pltpu.VMEM((width, f_out), F32),
+        ],
         compiler_params=pltpu.CompilerParams(vmem_limit_bytes=16 << 20),
-    )(me, agg, weight, cotangent)
+    )(me, weight, cotangent, *aggs)
+
+
+def turned(x, axis):
+    n = lax.axis_size(axis)
+    return [x] + [lax.ppermute(x, axis, [((i + by) % n, i) for i in range(n)]) for by in range(1, n)]
 
 
 def spread(x, axes):
@@ -184,11 +201,10 @@
 
 
 def shards(features, tile_vals, tile_cols, tile_count, weight, cotangent):
-    groups = lax.axis_size("col")
     slots = slots_of(tile_cols, tile_count, tile_vals.shape[0])
     pieces, whole_weight = halo(features, weight)
-    aggregated = tiles(pieces, slots, tile_vals, groups)
-    activated, part = dense(exchanged(aggregated, "col"), whole_weight, cotangent)
+    aggregated = tiles(pieces, slots, tile_vals)
+    activated, part = dense(turned(aggregated, "col"), whole_weight, cotangent)
     return activated, summed_over_row(part)
 
 

time: 133 us -> 134 us (level)
  starting transfers between devices: 32.6 us -> 38.7 us
  blocking collectives: 57.8 us -> 55.7 us
  waiting for transfers between devices: 28.2 us -> 26.5 us
    all_to_all x2 -> x1, waiting for transfers between devices: 22.9 us -> 3.44 us  [exchanged(): return lax.all_to_all(x, axes, 0, 0, tiled=True)]
    ppermute x0 -> x3, waiting for transfers between devices: none -> 16.9 us  [turned(): lax.ppermute(x, axis, [((i + by) % n, i) for i in range(n)])]
    ppermute x0 -> x3, starting transfers between devices: none -> 9.51 us  [turned(): lax.ppermute(x, axis, [((i + by) % n, i) for i in range(n)])]
    all_to_all x2 -> x1, starting transfers between devices: 7 us -> 3.6 us  [exchanged(): return lax.all_to_all(x, axes, 0, 0, tiled=True)]
    all_to_all x3, blocking collectives: 57.8 us -> 55.7 us  [exchanged(): return lax.all_to_all(x, axes, 0, 0, tiled=True)]
  transfers between devices with their start and end apart: 7 -> 9, of which waited for: 6 -> 8; matrix products, arithmetic and copies ran while one was open for 2% -> 2% of each run, Pallas kernels for 0% -> 0%
where the time goes in v8:
time: 134 us
  blocking collectives  55.7 us (42%)
  starting transfers between devices  38.7 us (29%)
  waiting for transfers between devices  26.5 us (20%)
  Pallas kernels  6.42 us (5%)
  other arithmetic  2.56 us (2%)
  local copies, waits for them, and re-layouts  2.28 us (2%)
  between operations  1.43 us (1%)
    all_to_all x3, blocking collectives, exchanged(): return lax.all_to_all(x, axes, 0, 0, tiled=True)  55.7 us
    ppermute x3, starting transfers between devices, swapped(): return lax.ppermute(x, 'core', [(0, 1), (1, 0)])  23 us
    ppermute x3, waiting for transfers between devices, turned(): lax.ppermute(x, axis, [((i + by) % n, i) for i in range(n)])  16.9 us
    ppermute x3, starting transfers between devices, turned(): lax.ppermute(x, axis, [((i + by) % n, i) for i in range(n)])  9.51 us
    ppermute x2, waiting for transfers between devices, passed_on(): return lax.ppermute(x, ROW, up + down)  4.43 us
    pallas_call x1, Pallas kernels, tiles(): pl.pallas_call(functools.partial(tiles_kernel, starts), out_shape=jax.Sha...  3.9 us
    all_to_all x1, starting transfers between devices, exchanged(): return lax.all_to_all(x, axes, 0, 0, tiled=True)  3.6 us
    all_to_all x1, waiting for transfers between devices, exchanged(): return lax.all_to_all(x, axes, 0, 0, tiled=True)  3.44 us
  transfers between devices with their start and end apart: 9, of which 8 were waited for; matrix products, arithmetic and copies ran while one was open for 2% of the time, Pallas kernels for 0%

profile of v8, /device:TPU:1, one launch (start us, length us, event | category | flops | bytes accessed | tf_op | source)
XLA Modules:
  0.0 133.7 jit_solution(15773424112018617332)
XLA Ops:
  0.6 16.1 %collective-permute-start = (bf16[1024,128]{1,0:T(8,128)(2,1)}, bf16[1024,128]{1,0:T(8,128)(2,1)S(1)}, u32[]{:S(2)}, u32[]{:S(2)}) collective-permute-start(bf16[1024,128]{1,0:T(8,128)(2,1)} %param.6), channel_id=1, source_target_pairs={{0,4},{4,0},{1,5},{5,1},{2,6},{6,2},{3,7},{7,3},{8,12},{12,8},{9,1... | collective-permute-start | bytes 786440 | tf_op jit(solution)/shard_map/ppermute | solution.py:18
  16.7 1.4 %collective-permute-done = bf16[1024,128]{1,0:T(8,128)(2,1)S(1)} collective-permute-done((bf16[1024,128]{1,0:T(8,128)(2,1)}, bf16[1024,128]{1,0:T(8,128)(2,1)S(1)}, u32[]{:S(2)}, u32[]{:S(2)}) %collective-permute-start) | collective-permute-done | bytes 262176 | tf_op jit(solution)/shard_map/ppermute | solution.py:18
  18.1 1.0 pad_maximum_fusion
  19.1 1.3 collective-permute-start.1
  20.4 1.7 %broadcast_in_dim.19 = bf16[4,128,512]{2,1,0:T(8,128)(2,1)} broadcast(bf16[128,512]{1,0:T(8,128)(2,1)} %param.10), dimensions={1,2} | broadcast | bytes 655360 | tf_op jit(solution)/shard_map/broadcast_in_dim | solution.py:187
  22.1 3.6 %all-to-all-start = ((bf16[4,128,512]{2,1,0:T(8,128)(2,1)}), bf16[4,128,512]{2,1,0:T(8,128)(2,1)S(1)}, u32[]{:S(2)}, u32[]{:S(2)}) async-start(bf16[4,128,512]{2,1,0:T(8,128)(2,1)} %broadcast_in_dim.19), calls=%async_computation | async-start | bytes 1048576 | tf_op jit(solution)/shard_map/all_to_all | solution.py:191
  25.7 3.4 %collective-permute-done.1 = bf16[2,1024,128]{2,1,0:T(8,128)(2,1)} collective-permute-done((bf16[2,1024,128]{2,1,0:T(8,128)(2,1)S(1)}, bf16[2,1024,128]{2,1,0:T(8,128)(2,1)}, u32[]{:S(2)}, u32[]{:S(2)}) %collective-permute-start.1) | collective-permute-done | bytes 524320 | tf_op jit(solution)/shard_map/ppermute | solution.py:25
  29.1 1.3 collective-permute-start.2
  30.4 3.5 %collective-permute-start.3 = (bf16[2,1024,128]{2,1,0:T(8,128)(2,1)}, bf16[2,1024,128]{2,1,0:T(8,128)(2,1)S(1)}, u32[]{:S(2)}, u32[]{:S(2)}) collective-permute-start(bf16[2,1024,128]{2,1,0:T(8,128)(2,1)} %collective-permute-done.1), channel_id=1, source_target_pairs={{0,4},{4,0},{1,5},{5,1},{2,6},{6,2},{3,7},{7,3},{8,12},{12,8},{9,1... | collective-permute-start | bytes 1572872 | tf_op jit(solution)/shard_map/ppermute | solution.py:18
  33.8 3.4 %all-to-all-done = bf16[4,128,512]{2,1,0:T(8,128)(2,1)S(1)} async-done(((bf16[4,128,512]{2,1,0:T(8,128)(2,1)}), bf16[4,128,512]{2,1,0:T(8,128)(2,1)S(1)}, u32[]{:S(2)}, u32[]{:S(2)}) %all-to-all-start) | async-done | bytes 524320 | tf_op jit(solution)/shard_map/all_to_all | solution.py:191
  38.5 1.0 collective-permute-done.2
  39.5 3.5 %collective-permute-start.4 = (bf16[1024,128]{1,0:T(8,128)(2,1)S(1)}, bf16[1024,128]{1,0:T(8,128)(2,1)S(1)}, u32[]{:S(2)}, u32[]{:S(2)}) collective-permute-start(bf16[1024,128]{1,0:T(8,128)(2,1)S(1)} %fusion), channel_id=1, source_target_pairs={{0,4},{4,0},{1,5},{5,1},{2,6},{6,2},{3,7},{7,3},{8,12},{12,8},{9,1... | collective-permute-start | bytes 786440 | tf_op jit(solution)/shard_map/ppermute | solution.py:18
  43.1 0.8 fusion.4.slots
  44.2 3.9 %shard_map.77.refs_0_ = bf16[1024,128]{1,0:T(8,128)(2,1)S(1)} custom-call(s32[8,16]{1,0:T(8,128)S(1)} %fusion.4.slots, bf16[8,128,128]{2,1,0:T(8,128)(2,1)} %bitcast.25, bf16[8,128,128]{2,1,0:T(8,128)(2,1)S(1)} %bitcast.20, bf16[16,128,128]{2,1,0:T(8,128)(2,1)} %bitcast.6.refs_2_, bf16[16,128,128]{2,1,0:T(8,128)(2,1)S(1)} %bitcast.18, ...), custom_call_target="tpu_custom_call" | custom-call | flops 536870912 | bytes 7340032 | tf_op jit(solution)/shard_map/pallas_call | solution.py:96
  48.1 3.6 %collective-permute-start.5 = (bf16[1024,128]{1,0:T(8,128)(2,1)S(1)}, bf16[1024,128]{1,0:T(8,128)(2,1)S(1)}, u32[]{:S(2)}, u32[]{:S(2)}) collective-permute-start(bf16[1024,128]{1,0:T(8,128)(2,1)S(1)} %shard_map.77.refs_0_), channel_id=1, source_target_pairs={{1,0},{2,1},{3,2},{0,3},{5,4},{6,5},{7,6},{4,7},{9,8},{10,9},{11,1... | collective-permute-start | bytes 786440 | tf_op jit(solution)/shard_map/ppermute | solution.py:182
  51.7 3.8 %collective-permute-start.6 = (bf16[1024,128]{1,0:T(8,128)(2,1)S(1)}, bf16[1024,128]{1,0:T(8,128)(2,1)S(1)}, u32[]{:S(2)}, u32[]{:S(2)}) collective-permute-start(bf16[1024,128]{1,0:T(8,128)(2,1)S(1)} %shard_map.77.refs_0_), channel_id=1, source_target_pairs={{2,0},{3,1},{0,2},{1,3},{6,4},{7,5},{4,6},{5,7},{10,8},{11,9},{8,1... | collective-permute-start | bytes 786440 | tf_op jit(solution)/shard_map/ppermute | solution.py:182
  55.5 2.1 %collective-permute-start.7 = (bf16[1024,128]{1,0:T(8,128)(2,1)S(1)}, bf16[1024,128]{1,0:T(8,128)(2,1)S(1)}, u32[]{:S(2)}, u32[]{:S(2)}) collective-permute-start(bf16[1024,128]{1,0:T(8,128)(2,1)S(1)} %shard_map.77.refs_0_), channel_id=1, source_target_pairs={{3,0},{0,1},{1,2},{2,3},{7,4},{4,5},{5,6},{6,7},{11,8},{8,9},{9,10... | collective-permute-start | bytes 786440 | tf_op jit(solution)/shard_map/ppermute | solution.py:182
  57.6 0.8 collective-permute-done.5.refs_1_
  58.4 12.7 %collective-permute-done.6.refs_2_ = bf16[1024,128]{1,0:T(8,128)(2,1)S(1)} collective-permute-done((bf16[1024,128]{1,0:T(8,128)(2,1)S(1)}, bf16[1024,128]{1,0:T(8,128)(2,1)S(1)}, u32[]{:S(2)}, u32[]{:S(2)}) %collective-permute-start.6) | collective-permute-done | bytes 262176 | tf_op jit(solution)/shard_map/ppermute | solution.py:182
  71.1 3.5 %collective-permute-done.7.refs_3_ = bf16[1024,128]{1,0:T(8,128)(2,1)S(1)} collective-permute-done((bf16[1024,128]{1,0:T(8,128)(2,1)S(1)}, bf16[1024,128]{1,0:T(8,128)(2,1)S(1)}, u32[]{:S(2)}, u32[]{:S(2)}) %collective-permute-start.7) | collective-permute-done | bytes 262176 | tf_op jit(solution)/shard_map/ppermute | solution.py:182
  74.6 2.5 %shard_map.78 = (bf16[1024,128]{1,0:T(8,128)(2,1)}, bf16[128,512]{1,0:T(8,128)(2,1)S(1)}) custom-call(s32[1]{0:T(128)} %bitcast.me, bf16[512,512]{1,0:T(8,128)(2,1)S(1)} %bitcast.17, bf16[1024,512]{1,0:T(8,128)(2,1)S(1)} %copy-done, bf16[1024,128]{1,0:T(8,128)(2,1)S(1)} %shard_map.77.refs_0_, bf16[1024,128]{1,0:T(8,128)(2,1)S(1)} %collective-permute-done.5.refs_1_, ...), custom_call_target="tpu_custom_call" | custom-call | tf_op jit(solution)/shard_map/pallas_call | solution.py:154
  77.1 30.6 %all_to_all.20 = bf16[16,8,512]{2,1,0:T(8,128)(2,1)S(1)} all-to-all(bf16[16,8,512]{2,1,0:T(8,128)(2,1)S(1)} %bitcast.23), channel_id=1, replica_groups=mesh['y_lo'=2,'x'=8,'z'=8,'core'=2,'col'=4] {'z','core'}, dimensions={0} | all-to-all | bytes 262144 | tf_op jit(solution)/shard_map/all_to_all | solution.py:191
  107.8 12.0 %all_to_all.21 = bf16[16,8,512]{2,1,0:T(8,128)(2,1)S(1)} all-to-all(bf16[16,8,512]{2,1,0:T(8,128)(2,1)S(1)} %broadcast_in_dim.21), channel_id=1, replica_groups=mesh['y_lo'=2,'x'=8,'z'=8,'core'=2,'col'=4] {'y_lo','x'}, dimensions={0} | all-to-all | bytes 262144 | tf_op jit(solution)/shard_map/all_to_all | solution.py:191
  119.9 13.1 %all_to_all.22 = bf16[16,8,512]{2,1,0:T(8,128)(2,1)S(1)} all-to-all(bf16[16,8,512]{2,1,0:T(8,128)(2,1)S(1)} %broadcast_in_dim.22), channel_id=1, replica_groups=mesh['y_lo'=2,'x'=8,'z'=8,'core'=2,'col'=4] {'z','core'}, dimensions={0} | all-to-all | bytes 262144 | tf_op jit(solution)/shard_map/all_to_all | solution.py:191
  (11 shorter events, 1.7 us)
Async XLA Ops:
  0.6 17.4 %collective-permute-start = (bf16[1024,128]{1,0:T(8,128)(2,1)}, bf16[1024,128]{1,0:T(8,128)(2,1)S(1)}, u32[]{:S(2)}, u32[]{:S(2)}) collective-permute-start(bf16[1024,128]{1,0:T(8,128)(2,1)} %param.6), channel_id=1, source_target_pairs={{0,4},{4,0},{1,5},{5,1},{2,6},{6,2},{3,7},{7,3},{8,12},{12,8},{9,1... | collective-permute-start | bytes 786440 | tf_op jit(solution)/shard_map/ppermute | solution.py:18
  19.1 10.0 %collective-permute-start.1 = (bf16[2,1024,128]{2,1,0:T(8,128)(2,1)S(1)}, bf16[2,1024,128]{2,1,0:T(8,128)(2,1)}, u32[]{:S(2)}, u32[]{:S(2)}) collective-permute-start(bf16[2,1024,128]{2,1,0:T(8,128)(2,1)S(1)} %pad_maximum_fusion), channel_id=1, source_target_pairs={{0,8},{8,16},{16,24},{24,32},{32,40},{40,48},{48,56},{56,64},{64,7... | collective-permute-start | bytes 1572872 | tf_op jit(solution)/shard_map/ppermute | solution.py:25
  22.1 52.5 %copy-start = (bf16[1024,512]{1,0:T(8,128)(2,1)S(1)}, bf16[1024,512]{1,0:T(8,128)(2,1)}, u32[]{:S(2)}) copy-start(bf16[1024,512]{1,0:T(8,128)(2,1)} %cotangent.1) | copy-start | bytes 3145732
  22.1 15.2 %all-to-all-start = ((bf16[4,128,512]{2,1,0:T(8,128)(2,1)}), bf16[4,128,512]{2,1,0:T(8,128)(2,1)S(1)}, u32[]{:S(2)}, u32[]{:S(2)}) async-start(bf16[4,128,512]{2,1,0:T(8,128)(2,1)} %broadcast_in_dim.19), calls=%async_computation | async-start | bytes 1048576 | tf_op jit(solution)/shard_map/all_to_all | solution.py:191
  29.1 10.4 %collective-permute-start.2 = (bf16[2,1024,128]{2,1,0:T(8,128)(2,1)}, bf16[2,1024,128]{2,1,0:T(8,128)(2,1)S(1)}, u32[]{:S(2)}, u32[]{:S(2)}) collective-permute-start(bf16[2,1024,128]{2,1,0:T(8,128)(2,1)} %collective-permute-done.1), channel_id=1, source_target_pairs={{0,8},{8,16},{16,24},{24,32},{32,40},{40,48},{48,56},{56,64},{64,7... | collective-permute-start | bytes 1572872 | tf_op jit(solution)/shard_map/ppermute | solution.py:25
  30.4 13.5 %collective-permute-start.3 = (bf16[2,1024,128]{2,1,0:T(8,128)(2,1)}, bf16[2,1024,128]{2,1,0:T(8,128)(2,1)S(1)}, u32[]{:S(2)}, u32[]{:S(2)}) collective-permute-start(bf16[2,1024,128]{2,1,0:T(8,128)(2,1)} %collective-permute-done.1), channel_id=1, source_target_pairs={{0,4},{4,0},{1,5},{5,1},{2,6},{6,2},{3,7},{7,3},{8,12},{12,8},{9,1... | collective-permute-start | bytes 1572872 | tf_op jit(solution)/shard_map/ppermute | solution.py:18
  39.5 4.7 %collective-permute-start.4 = (bf16[1024,128]{1,0:T(8,128)(2,1)S(1)}, bf16[1024,128]{1,0:T(8,128)(2,1)S(1)}, u32[]{:S(2)}, u32[]{:S(2)}) collective-permute-start(bf16[1024,128]{1,0:T(8,128)(2,1)S(1)} %fusion), channel_id=1, source_target_pairs={{0,4},{4,0},{1,5},{5,1},{2,6},{6,2},{3,7},{7,3},{8,12},{12,8},{9,1... | collective-permute-start | bytes 786440 | tf_op jit(solution)/shard_map/ppermute | solution.py:18
  48.1 10.3 %collective-permute-start.5 = (bf16[1024,128]{1,0:T(8,128)(2,1)S(1)}, bf16[1024,128]{1,0:T(8,128)(2,1)S(1)}, u32[]{:S(2)}, u32[]{:S(2)}) collective-permute-start(bf16[1024,128]{1,0:T(8,128)(2,1)S(1)} %shard_map.77.refs_0_), channel_id=1, source_target_pairs={{1,0},{2,1},{3,2},{0,3},{5,4},{6,5},{7,6},{4,7},{9,8},{10,9},{11,1... | collective-permute-start | bytes 786440 | tf_op jit(solution)/shard_map/ppermute | solution.py:182
  51.7 19.4 %collective-permute-start.6 = (bf16[1024,128]{1,0:T(8,128)(2,1)S(1)}, bf16[1024,128]{1,0:T(8,128)(2,1)S(1)}, u32[]{:S(2)}, u32[]{:S(2)}) collective-permute-start(bf16[1024,128]{1,0:T(8,128)(2,1)S(1)} %shard_map.77.refs_0_), channel_id=1, source_target_pairs={{2,0},{3,1},{0,2},{1,3},{6,4},{7,5},{4,6},{5,7},{10,8},{11,9},{8,1... | collective-permute-start | bytes 786440 | tf_op jit(solution)/shard_map/ppermute | solution.py:182
  55.5 19.1 %collective-permute-start.7 = (bf16[1024,128]{1,0:T(8,128)(2,1)S(1)}, bf16[1024,128]{1,0:T(8,128)(2,1)S(1)}, u32[]{:S(2)}, u32[]{:S(2)}) collective-permute-start(bf16[1024,128]{1,0:T(8,128)(2,1)S(1)} %shard_map.77.refs_0_), channel_id=1, source_target_pairs={{3,0},{0,1},{1,2},{2,3},{7,4},{4,5},{5,6},{6,7},{11,8},{8,9},{9,10... | collective-permute-start | bytes 786440 | tf_op jit(solution)/shard_map/ppermute | solution.py:182

commit v9 on v5

--- a/solution.py
+++ b/solution.py
@@ -64,8 +64,11 @@
     ]
     for copy in copies:
         copy.start()
+    span = blocks // vals_sems.shape[0]
+    parts = [pl.ds(i * span, span) for i in range(vals_sems.shape[0])]
     fetches = [
-        pltpu.make_async_copy(vals_hbm.at[b], vals.at[b], vals_sems.at[b]) for b in range(blocks)
+        pltpu.make_async_copy(vals_hbm.at[part], vals.at[part], vals_sems.at[i])
+        for i, part in enumerate(parts)
     ]
     for fetch in fetches:
         fetch.start()
@@ -73,7 +76,8 @@
     for copy in copies:
         copy.wait()
     for b in range(blocks):
-        fetches[b].wait()
+        if b % span == 0:
+            fetches[b // span].wait()
         total = jnp.zeros((tile, cols), F32)
         for t in range(0, count, 2):
             pair = jnp.concatenate([vals[b, t], vals[b, t + 1]], axis=1)
@@ -103,7 +107,7 @@
             pltpu.VMEM((9 * blocks + 1, tile, cols), BF16),
             pltpu.VMEM(tile_vals.shape, BF16),
             pltpu.SemaphoreType.DMA((len(arrays),)),
-            pltpu.SemaphoreType.DMA((blocks,)),
+            pltpu.SemaphoreType.DMA((blocks // 2,)),
         ],
         compiler_params=pltpu.CompilerParams(vmem_limit_bytes=16 << 20),
         cost_estimate=pl.CostEstimate(
@@ -140,7 +144,7 @@
 def dense(agg, weight, cotangent):
     groups, rows, width = agg.shape
     f_out = weight.shape[1]
-    block = 256
+    block = 512
     me = lax.axis_index("col").astype(jnp.int32)[None]
     return pl.pallas_call(
         dense_kernel,

time: 134 us -> 132 us (0.985)
  Pallas kernels: 9.35 us -> 7.69 us
where the time goes in v9:
time: 132 us
  blocking collectives  54 us (41%)
  starting transfers between devices  42.7 us (32%)
  waiting for transfers between devices  22.4 us (17%)
  Pallas kernels  7.69 us (6%)
  local copies, waits for them, and re-layouts  2.47 us (2%)
  other arithmetic  1.59 us (1%)
    all_to_all x3, blocking collectives, exchanged(): return lax.all_to_all(x, axes, 0, 0, tiled=True)  54 us
    ppermute x3, starting transfers between devices, swapped(): return lax.ppermute(x, 'core', [(0, 1), (1, 0)])  27.1 us
    all_to_all x2, waiting for transfers between devices, exchanged(): return lax.all_to_all(x, axes, 0, 0, tiled=True)  19 us
    all_to_all x2, starting transfers between devices, exchanged(): return lax.all_to_all(x, axes, 0, 0, tiled=True)  10.4 us
    ppermute x4, starting transfers between devices, passed_on(): return lax.ppermute(x, ROW, up + down)  5.16 us
    pallas_call x1, Pallas kernels, tiles(): pl.pallas_call(functools.partial(tiles_kernel, starts), out_shape=jax.Sha...  5.13 us
  transfers between devices with their start and end apart: 9, of which 5 were waited for; matrix products, arithmetic and copies ran while one was open for 2% of the time, Pallas kernels for 0%

profile of v9, /device:TPU:1, one launch (start us, length us, event | category | flops | bytes accessed | tf_op | source)
XLA Modules:
  0.0 131.6 jit_solution(9355787013779052181)
XLA Ops:
  0.6 16.1 %collective-permute-start = (bf16[1024,128]{1,0:T(8,128)(2,1)}, bf16[1024,128]{1,0:T(8,128)(2,1)S(1)}, u32[]{:S(2)}, u32[]{:S(2)}) collective-permute-start(bf16[1024,128]{1,0:T(8,128)(2,1)} %param.6), channel_id=1, source_target_pairs={{0,4},{4,0},{1,5},{5,1},{2,6},{6,2},{3,7},{7,3},{8,12},{12,8},{9,1... | collective-permute-start | bytes 786440 | tf_op jit(solution)/shard_map/ppermute | solution.py:18
  16.7 1.4 %collective-permute-done = bf16[1024,128]{1,0:T(8,128)(2,1)S(1)} collective-permute-done((bf16[1024,128]{1,0:T(8,128)(2,1)}, bf16[1024,128]{1,0:T(8,128)(2,1)S(1)}, u32[]{:S(2)}, u32[]{:S(2)}) %collective-permute-start) | collective-permute-done | bytes 262176 | tf_op jit(solution)/shard_map/ppermute | solution.py:18
  18.1 1.3 collective-permute-start.2
  19.3 1.3 collective-permute-start.1
  20.6 1.7 %broadcast_in_dim.20 = bf16[4,128,512]{2,1,0:T(8,128)(2,1)} broadcast(bf16[128,512]{1,0:T(8,128)(2,1)} %param.10), dimensions={1,2} | broadcast | bytes 655360 | tf_op jit(solution)/shard_map/broadcast_in_dim | solution.py:173
  22.4 3.5 %all-to-all-start = ((bf16[4,128,512]{2,1,0:T(8,128)(2,1)}), bf16[4,128,512]{2,1,0:T(8,128)(2,1)S(1)}, u32[]{:S(2)}, u32[]{:S(2)}) async-start(bf16[4,128,512]{2,1,0:T(8,128)(2,1)} %broadcast_in_dim.20), calls=%async_computation | async-start | bytes 1048576 | tf_op jit(solution)/shard_map/all_to_all | solution.py:177
  25.9 1.3 collective-permute-start.4
  27.2 0.8 collective-permute-done.1
  28.0 0.1 pad_maximum_fusion
  28.0 4.6 %collective-permute-start.5 = (bf16[2,1024,128]{2,1,0:T(8,128)(2,1)S(1)}, bf16[2,1024,128]{2,1,0:T(8,128)(2,1)S(1)}, u32[]{:S(2)}, u32[]{:S(2)}) collective-permute-start(bf16[2,1024,128]{2,1,0:T(8,128)(2,1)S(1)} %pad_maximum_fusion), channel_id=1, source_target_pairs={{0,4},{4,0},{1,5},{5,1},{2,6},{6,2},{3,7},{7,3},{8,12},{12,8},{9,1... | collective-permute-start | bytes 1572872 | tf_op jit(solution)/shard_map/ppermute | solution.py:18
  32.6 1.3 collective-permute-start.3
  33.9 0.6 collective-permute-done.4
  34.5 6.4 %collective-permute-start.6 = (bf16[1024,128]{1,0:T(8,128)(2,1)S(1)}, bf16[1024,128]{1,0:T(8,128)(2,1)S(1)}, u32[]{:S(2)}, u32[]{:S(2)}) collective-permute-start(bf16[1024,128]{1,0:T(8,128)(2,1)S(1)} %collective-permute-done.4), channel_id=1, source_target_pairs={{0,4},{4,0},{1,5},{5,1},{2,6},{6,2},{3,7},{7,3},{8,12},{12,8},{9,1... | collective-permute-start | bytes 786440 | tf_op jit(solution)/shard_map/ppermute | solution.py:18
  41.0 0.8 fusion.3.slots
  41.8 0.7 collective-permute-done.3
  42.5 0.7 copy-done.1
  43.2 5.1 %shard_map.77 = bf16[4,1024,128]{2,1,0:T(8,128)(2,1)} custom-call(s32[8,16]{1,0:T(8,128)S(1)} %fusion.3.slots, bf16[8,128,128]{2,1,0:T(8,128)(2,1)} %bitcast.26, bf16[8,128,128]{2,1,0:T(8,128)(2,1)S(1)} %bitcast.22, bf16[8,128,128]{2,1,0:T(8,128)(2,1)S(1)} %bitcast.20, bf16[8,128,128]{2,1,0:T(8,128)(2,1)S(1)} %bitcast.18, bf16[8,128,128]{2,1,0:T(8,128)(2,1)S(1)} %bitcast.24, ...), custom_call_target="tpu_custom_call" | custom-call | flops 536870912 | bytes 7340032 | tf_op jit(solution)/shard_map/pallas_call | solution.py:101
  48.4 6.9 %all-to-all-start.1 = ((bf16[4,1024,128]{2,1,0:T(8,128)(2,1)}), bf16[4,1024,128]{2,1,0:T(8,128)(2,1)S(1)}, u32[]{:S(2)}, u32[]{:S(2)}) async-start(bf16[4,1024,128]{2,1,0:T(8,128)(2,1)} %shard_map.77), calls=%async_computation.1 | async-start | bytes 2097152 | tf_op jit(solution)/shard_map/all_to_all | solution.py:177
  55.3 19.0 %all-to-all-done.1.agg = bf16[4,1024,128]{2,1,0:T(8,128)(2,1)S(1)} async-done(((bf16[4,1024,128]{2,1,0:T(8,128)(2,1)}), bf16[4,1024,128]{2,1,0:T(8,128)(2,1)S(1)}, u32[]{:S(2)}, u32[]{:S(2)}) %all-to-all-start.1) | async-done | bytes 1048608 | tf_op jit(solution)/shard_map/all_to_all | solution.py:177
  74.3 2.6 %shard_map.78 = (bf16[1024,128]{1,0:T(8,128)(2,1)}, bf16[128,512]{1,0:T(8,128)(2,1)S(1)}) custom-call(s32[1]{0:T(128)} %bitcast.me, bf16[4,1024,128]{2,1,0:T(8,128)(2,1)S(1)} %all-to-all-done.1.agg, bf16[512,512]{1,0:T(8,128)(2,1)S(1)} %bitcast.16, bf16[1024,512]{1,0:T(8,128)(2,1)S(1)} %copy-done), custom_call_target="tpu_custom_call" | custom-call | tf_op jit(solution)/shard_map/pallas_call | solution.py:149
  76.8 25.9 %all_to_all.25 = bf16[16,8,512]{2,1,0:T(8,128)(2,1)S(1)} all-to-all(bf16[16,8,512]{2,1,0:T(8,128)(2,1)S(1)} %bitcast.25), channel_id=1, replica_groups=mesh['y_lo'=2,'x'=8,'z'=8,'core'=2,'col'=4] {'z','core'}, dimensions={0} | all-to-all | bytes 262144 | tf_op jit(solution)/shard_map/all_to_all | solution.py:177
  102.8 15.0 %all_to_all.26 = bf16[16,8,512]{2,1,0:T(8,128)(2,1)S(1)} all-to-all(bf16[16,8,512]{2,1,0:T(8,128)(2,1)S(1)} %broadcast_in_dim.21), channel_id=1, replica_groups=mesh['y_lo'=2,'x'=8,'z'=8,'core'=2,'col'=4] {'y_lo','x'}, dimensions={0} | all-to-all | bytes 262144 | tf_op jit(solution)/shard_map/all_to_all | solution.py:177
  117.8 13.1 %all_to_all.27 = bf16[16,8,512]{2,1,0:T(8,128)(2,1)S(1)} all-to-all(bf16[16,8,512]{2,1,0:T(8,128)(2,1)S(1)} %broadcast_in_dim.22), channel_id=1, replica_groups=mesh['y_lo'=2,'x'=8,'z'=8,'core'=2,'col'=4] {'z','core'}, dimensions={0} | all-to-all | bytes 262144 | tf_op jit(solution)/shard_map/all_to_all | solution.py:177
  130.9 0.7 bitcast_convert_fusion
  (11 shorter events, 0.1 us)
Async XLA Ops:
  0.6 17.4 %collective-permute-start = (bf16[1024,128]{1,0:T(8,128)(2,1)}, bf16[1024,128]{1,0:T(8,128)(2,1)S(1)}, u32[]{:S(2)}, u32[]{:S(2)}) collective-permute-start(bf16[1024,128]{1,0:T(8,128)(2,1)} %param.6), channel_id=1, source_target_pairs={{0,4},{4,0},{1,5},{5,1},{2,6},{6,2},{3,7},{7,3},{8,12},{12,8},{9,1... | collective-permute-start | bytes 786440 | tf_op jit(solution)/shard_map/ppermute | solution.py:18
  18.1 7.8 %collective-permute-start.2 = (bf16[1024,128]{1,0:T(8,128)(2,1)S(1)}, bf16[1024,128]{1,0:T(8,128)(2,1)S(1)}, u32[]{:S(2)}, u32[]{:S(2)}) collective-permute-start(bf16[1024,128]{1,0:T(8,128)(2,1)S(1)} %collective-permute-done), channel_id=1, source_target_pairs={{0,8},{8,16},{16,24},{24,32},{32,40},{40,48},{48,56},{56,64},{64,7... | collective-permute-start | bytes 786440 | tf_op jit(solution)/shard_map/ppermute | solution.py:25
  19.3 8.6 %collective-permute-start.1 = (bf16[1024,128]{1,0:T(8,128)(2,1)}, bf16[1024,128]{1,0:T(8,128)(2,1)S(1)}, u32[]{:S(2)}, u32[]{:S(2)}) collective-permute-start(bf16[1024,128]{1,0:T(8,128)(2,1)} %param.6), channel_id=1, source_target_pairs={{0,8},{8,16},{16,24},{24,32},{32,40},{40,48},{48,56},{56,64},{64,7... | collective-permute-start | bytes 786440 | tf_op jit(solution)/shard_map/ppermute | solution.py:25
  22.4 20.1 %all-to-all-start = ((bf16[4,128,512]{2,1,0:T(8,128)(2,1)}), bf16[4,128,512]{2,1,0:T(8,128)(2,1)S(1)}, u32[]{:S(2)}, u32[]{:S(2)}) async-start(bf16[4,128,512]{2,1,0:T(8,128)(2,1)} %broadcast_in_dim.20), calls=%async_computation | async-start | bytes 1048576 | tf_op jit(solution)/shard_map/all_to_all | solution.py:177
  25.9 8.7 %collective-permute-start.4 = (bf16[1024,128]{1,0:T(8,128)(2,1)S(1)}, bf16[1024,128]{1,0:T(8,128)(2,1)S(1)}, u32[]{:S(2)}, u32[]{:S(2)}) collective-permute-start(bf16[1024,128]{1,0:T(8,128)(2,1)S(1)} %collective-permute-done.2), channel_id=1, source_target_pairs={{0,8},{8,16},{16,24},{24,32},{32,40},{40,48},{48,56},{56,64},{64,7... | collective-permute-start | bytes 786440 | tf_op jit(solution)/shard_map/ppermute | solution.py:25
  28.0 14.5 %collective-permute-start.5 = (bf16[2,1024,128]{2,1,0:T(8,128)(2,1)S(1)}, bf16[2,1024,128]{2,1,0:T(8,128)(2,1)S(1)}, u32[]{:S(2)}, u32[]{:S(2)}) collective-permute-start(bf16[2,1024,128]{2,1,0:T(8,128)(2,1)S(1)} %pad_maximum_fusion), channel_id=1, source_target_pairs={{0,4},{4,0},{1,5},{5,1},{2,6},{6,2},{3,7},{7,3},{8,12},{12,8},{9,1... | collective-permute-start | bytes 1572872 | tf_op jit(solution)/shard_map/ppermute | solution.py:18
  32.6 9.9 %collective-permute-start.3 = (bf16[1024,128]{1,0:T(8,128)(2,1)S(1)}, bf16[1024,128]{1,0:T(8,128)(2,1)S(1)}, u32[]{:S(2)}, u32[]{:S(2)}) collective-permute-start(bf16[1024,128]{1,0:T(8,128)(2,1)S(1)} %collective-permute-done.1), channel_id=1, source_target_pairs={{0,8},{8,16},{16,24},{24,32},{32,40},{40,48},{48,56},{56,64},{64,7... | collective-permute-start | bytes 786440 | tf_op jit(solution)/shard_map/ppermute | solution.py:25
  34.5 8.0 %collective-permute-start.6 = (bf16[1024,128]{1,0:T(8,128)(2,1)S(1)}, bf16[1024,128]{1,0:T(8,128)(2,1)S(1)}, u32[]{:S(2)}, u32[]{:S(2)}) collective-permute-start(bf16[1024,128]{1,0:T(8,128)(2,1)S(1)} %collective-permute-done.4), channel_id=1, source_target_pairs={{0,4},{4,0},{1,5},{5,1},{2,6},{6,2},{3,7},{7,3},{8,12},{12,8},{9,1... | collective-permute-start | bytes 786440 | tf_op jit(solution)/shard_map/ppermute | solution.py:18
  42.5 0.7 copy-start.1
  43.2 31.0 %copy-start = (bf16[1024,512]{1,0:T(8,128)(2,1)S(1)}, bf16[1024,512]{1,0:T(8,128)(2,1)}, u32[]{:S(2)}) copy-start(bf16[1024,512]{1,0:T(8,128)(2,1)} %cotangent.1) | copy-start | bytes 3145732
  48.4 25.9 %all-to-all-start.1 = ((bf16[4,1024,128]{2,1,0:T(8,128)(2,1)}), bf16[4,1024,128]{2,1,0:T(8,128)(2,1)S(1)}, u32[]{:S(2)}, u32[]{:S(2)}) async-start(bf16[4,1024,128]{2,1,0:T(8,128)(2,1)} %shard_map.77), calls=%async_computation.1 | async-start | bytes 2097152 | tf_op jit(solution)/shard_map/all_to_all | solution.py:177
